TPU v7x, 32 devices: a whole 2x2x4 slice. The times are simulated.
32 devices in a mesh: section: 2 (over core), dp: 4 (over y, x), seq: 4 (over z).
Axes of the slice: x: 2, y: 2, z: 4, core: 2. Of those that a mesh axis runs over, the one named last changes fastest.
Arguments:
- layer_in: bfloat16 [2, 4, 1024, 1120], P(None, 'dp', 'seq'), may hold values from -6 to 6
- cotangent: bfloat16 [2, 4, 1024, 1120], P(None, 'dp', 'seq'), may hold values from -6 to 6
- lengths: int32 [2, 4], P(None, 'dp'), may hold values from 128 to 1024, as said below
- block_order: int32 [4], replicated, may hold values from 0 to 3, each once
- w_qkv: float32 [2, 1120, 3360], P('section', 'dp'), may hold values from -0.25 to 0.25
- w_out: float32 [2, 1120, 1120], P('section', 'dp'), may hold values from -1.5 to 1.5
- w_fc: float32 [2, 1120, 4480], P('section', 'dp'), may hold values from -0.1875 to 0.1875
- w_proj: float32 [2, 4480, 1120], P('section', 'dp'), may hold values from -0.09375 to 0.09375
- norm_gains: float32 [2, 2, 1120], P('section'), may hold values from 0.5 to 1.5
- norm_biases: float32 [2, 2, 1120], P('section'), may hold values from -1.5 to 1.5
Outputs:
- layer_out: bfloat16 [2, 2, 4, 1024, 1120], P('section', None, 'dp', 'seq')
- input_grad: bfloat16 [2, 2, 4, 1024, 1120], P('section', None, 'dp', 'seq')
- grad_qkv: float32 [2, 1120, 3360], P('section', 'dp')
- grad_out: float32 [2, 1120, 1120], P('section', 'dp')
- grad_fc: float32 [2, 1120, 4480], P('section', 'dp')
- grad_proj: float32 [2, 4480, 1120], P('section', 'dp')
- grad_gains: float32 [2, 2, 1120], P('section', None, 'dp')
- grad_biases: float32 [2, 2, 1120], P('section', None, 'dp')
Inputs may be any that keep to these rules, and one draw needn't show every extreme that they name: `lengths`: rows at positions at or past a cell's length are padding. For every cell index, one of the 2 micro-batches has a cell of full length 1024. `block_order`: each block index appears once.
All inputs are finite; a program needn't handle non-finite values.
Results may differ from a plain program's by a relative error of at most 0.02.
Values may be sent and summed in bfloat16 or wider, within the bound.
A program may use at most 384 MiB of HBM per device.

v0:
```python
import jax
import jax.numpy as jnp
from jax import lax
from jax.sharding import PartitionSpec as P

HEADS = 20
HEAD_DIM = 56


EPS = 1e-05
NEG = -1e30
group_heads = 4


def from_behind(block, axis, distance):
    devices = range(lax.axis_size(axis))
    route = [(i - distance, i) for i in devices if i - distance in devices]
    return lax.ppermute(block, axis, route)


def layer_norm(values, gain, bias):
    center = values - jnp.mean(values, axis=-1, keepdims=True)
    spread = jnp.mean(center * center, axis=-1, keepdims=True)
    return center * lax.rsqrt(spread + EPS) * gain + bias


def gelu_exact(values):
    return jax.nn.gelu(values, approximate=False)


def store_slot(buffers, elements, slot, live_slot):
    updated = []
    for buffer, element in zip(buffers, elements):
        former = lax.dynamic_index_in_dim(buffer, slot, 0, False)
        updated.append(
            lax.dynamic_update_index_in_dim(buffer, jnp.where(live_slot, element, former), slot, 0)
        )
    return tuple(updated)


def head_split(values, rows, groups, head_dim):
    return values.reshape(rows, groups, group_heads, head_dim).transpose(1, 2, 0, 3)


def head_join(values, rows, hidden_width):
    return values.transpose(2, 0, 1, 3).reshape(rows, hidden_width)


def on_device(
    layer_in, cotangent, lengths, block_order, w_qkv, w_out, w_fc, w_proj, norm_gains, norm_biases
):
    micro_count = layer_in.shape[0]
    tokens = layer_in.shape[2]
    hidden_width = layer_in.shape[3]
    ff_width = w_fc.shape[2]
    head_count = HEADS
    head_dim = HEAD_DIM
    groups = head_count // group_heads
    score_scale = head_dim ** (-0.5)
    blocks = lax.axis_size("seq")
    seq_len = tokens * blocks
    section_index = lax.axis_index("section")
    bf16 = jnp.bfloat16
    f32 = jnp.float32
    wqkv, wout, wfc, wproj = (
        lax.all_gather(w_qkv[0].astype(bf16), "dp", axis=0, tiled=True),
        lax.all_gather(w_out[0].astype(bf16), "dp", axis=0, tiled=True),
        lax.all_gather(w_fc[0].astype(bf16), "dp", axis=0, tiled=True),
        lax.all_gather(w_proj[0].astype(bf16), "dp", axis=0, tiled=True),
    )
    gains = norm_gains[0]
    biases = norm_biases[0]
    starts = block_order * tokens
    offsets = jnp.arange(tokens, dtype=jnp.int32)
    key_pos = (starts[:, None] + offsets[None, :]).reshape(seq_len)
    my_start = jnp.sum(
        jnp.where(jnp.arange(blocks, dtype=jnp.int32) == lax.axis_index("seq"), starts, 0)
    )
    my_pos = my_start + offsets
    cell_lengths = lengths[:, 0]

    def length_of(slot):
        return lax.dynamic_index_in_dim(cell_lengths, slot, 0, False)

    def allowed(limit):
        return (key_pos[None, :] <= my_pos[:, None]) & (key_pos[None, :] < limit)

    def forward(layer_input, mask):
        hidden_val = layer_input.astype(f32)
        normed = layer_norm(hidden_val, gains[0], biases[0]).astype(bf16)
        projected = jnp.dot(normed, wqkv, preferred_element_type=f32).astype(bf16)
        gathered = lax.all_gather(projected[:, hidden_width:], "seq", axis=0, tiled=True)
        queries = projected[:, :hidden_width].reshape(tokens, head_count, head_dim)
        keys = gathered[:, :hidden_width].reshape(seq_len, head_count, head_dim)
        values = gathered[:, hidden_width:].reshape(seq_len, head_count, head_dim)
        scores = jnp.einsum("qhd,khd->hqk", queries, keys, preferred_element_type=f32) * score_scale
        scores = jnp.where(mask[None], scores, NEG)
        row_peak = jnp.max(scores, axis=-1, keepdims=True)
        row_exp = jnp.exp(scores - row_peak)
        row_total = jnp.sum(row_exp, axis=-1, keepdims=True)
        attn_probs = (row_exp / row_total).astype(bf16)
        log_total = (row_peak + jnp.log(row_total))[..., 0]
        attended = (
            jnp.einsum("hqk,khd->qhd", attn_probs, values, preferred_element_type=f32)
            .reshape(tokens, hidden_width)
            .astype(bf16)
        )
        residual = hidden_val + jnp.dot(attended, wout, preferred_element_type=f32)
        second = layer_norm(residual, gains[1], biases[1]).astype(bf16)
        pre_act = jnp.dot(second, wfc, preferred_element_type=f32)
        activated = gelu_exact(pre_act).astype(bf16)
        result = (residual + jnp.dot(activated, wproj, preferred_element_type=f32)).astype(bf16)
        saved = (
            layer_input,
            normed,
            projected,
            log_total,
            attended,
            residual,
            second,
            pre_act,
            activated,
        )
        return (result, saved, gathered)

    saved_init = (
        jnp.zeros((micro_count, tokens, hidden_width), bf16),
        jnp.zeros((micro_count, tokens, hidden_width), bf16),
        jnp.zeros((micro_count, tokens, 3 * hidden_width), bf16),
        jnp.zeros((micro_count, head_count, tokens), f32),
        jnp.zeros((micro_count, tokens, hidden_width), bf16),
        jnp.zeros((micro_count, tokens, hidden_width), f32),
        jnp.zeros((micro_count, tokens, hidden_width), bf16),
        jnp.zeros((micro_count, tokens, ff_width), f32),
        jnp.zeros((micro_count, tokens, ff_width), bf16),
    )

    def forward_tick(step_number, state_in):
        previous, outputs, buffers = state_in
        incoming = from_behind(previous, "section", 1)
        slot_raw = step_number - section_index
        live_slot = (slot_raw >= 0) & (slot_raw < micro_count)
        slot = jnp.clip(slot_raw, 0, micro_count - 1)
        own_input = lax.dynamic_index_in_dim(layer_in[:, 0], slot, 0, False)
        layer_input = jnp.where(section_index == 0, own_input, incoming)
        result, saved, gathered = forward(layer_input, allowed(length_of(slot)))
        outputs = store_slot((outputs,), (result,), slot, live_slot)[0]
        buffers = store_slot(buffers, saved, slot, live_slot)
        return (result, outputs, buffers)

    forward_state = (
        jnp.zeros((tokens, hidden_width), bf16),
        jnp.zeros((micro_count, tokens, hidden_width), bf16),
        saved_init,
    )
    ignored, layer_results, buffers = lax.fori_loop(0, micro_count + 1, forward_tick, forward_state)

    def attention_back(projected, log_total, keys_all, mask, d_att):
        query_groups = head_split(projected[:, :hidden_width], tokens, groups, head_dim)
        key_groups = head_split(keys_all[:, :hidden_width], seq_len, groups, head_dim)
        value_groups = head_split(keys_all[:, hidden_width:], seq_len, groups, head_dim)
        grad_groups = head_split(d_att, tokens, groups, head_dim)
        lse_groups = log_total.reshape(groups, group_heads, tokens)

        def one_group(operands):
            group_q, group_k, group_v, group_d, group_lse = operands
            scores = (
                jnp.einsum("hqd,hkd->hqk", group_q, group_k, preferred_element_type=f32)
                * score_scale
            )
            scores = jnp.where(mask[None], scores, NEG)
            row_probs = jnp.exp(scores - group_lse[..., None])
            d_prob = jnp.einsum("hqd,hkd->hqk", group_d, group_v, preferred_element_type=f32)
            row_inner = jnp.sum(row_probs * d_prob, axis=-1)
            d_score = (row_probs * (d_prob - row_inner[..., None]) * score_scale).astype(bf16)
            d_query = jnp.einsum("hqk,hkd->hqd", d_score, group_k, preferred_element_type=f32)
            return (d_query, row_inner, row_probs.astype(bf16), d_score)

        d_query, row_inner, probs_low, score_grads = lax.map(
            one_group, (query_groups, key_groups, value_groups, grad_groups, lse_groups)
        )
        d_query = head_join(d_query, tokens, hidden_width)
        row_inner = row_inner.reshape(head_count, tokens)
        probs_low = probs_low.reshape(head_count, tokens, seq_len)
        score_grads = score_grads.reshape(head_count, tokens, seq_len)
        query_heads = projected[:, :hidden_width].reshape(tokens, head_count, head_dim)
        backward_heads = d_att.reshape(tokens, head_count, head_dim)
        d_key = jnp.einsum(
            "hqk,qhd->khd", score_grads, query_heads, preferred_element_type=f32
        ).reshape(lax.axis_size("seq") * tokens, hidden_width)
        d_value = jnp.einsum(
            "hqk,qhd->khd", probs_low, backward_heads, preferred_element_type=f32
        ).reshape(lax.axis_size("seq") * tokens, hidden_width)
        pair_grads = lax.psum_scatter(
            jnp.concatenate([d_key, d_value], axis=1).astype(jnp.bfloat16),
            "seq",
            scatter_dimension=0,
            tiled=True,
        ).astype(jnp.float32)
        return (d_query, pair_grads)

    def backward_tick(step_number, state_in):
        previous, grad_outputs, running_total = state_in
        incoming = from_behind(previous, "section", -1)
        slot_raw = step_number - 1 + section_index
        live_slot = (slot_raw >= 0) & (slot_raw < micro_count)
        slot = jnp.clip(slot_raw, 0, micro_count - 1)
        elements = tuple((lax.dynamic_index_in_dim(buffer, slot, 0, False) for buffer in buffers))
        (
            layer_input,
            normed,
            projected,
            log_total,
            attended,
            residual,
            second,
            pre_act,
            activated,
        ) = elements[:9]
        limit = length_of(slot)
        own_cot = lax.dynamic_index_in_dim(cotangent[:, 0], slot, 0, False)
        upstream = jnp.where(section_index == 1, own_cot, incoming).astype(f32)
        mlp_grad = upstream.astype(bf16)
        d_act = jnp.einsum("td,fd->tf", mlp_grad, wproj, preferred_element_type=f32)
        d_pre = jax.vjp(gelu_exact, pre_act)[1](d_act)[0].astype(bf16)
        d_second = jnp.einsum("tf,df->td", d_pre, wfc, preferred_element_type=f32)
        d_res_norm, g_gain_two, g_bias_two = jax.vjp(layer_norm, residual, gains[1], biases[1])[1](
            d_second
        )
        d_residual = upstream + d_res_norm
        branch_grad = d_residual.astype(bf16)
        d_att = jnp.einsum("te,de->td", branch_grad, wout, preferred_element_type=f32).astype(bf16)
        keys_all = lax.all_gather(projected[:, hidden_width:], "seq", axis=0, tiled=True)
        d_query, pair_grads = attention_back(projected, log_total, keys_all, allowed(limit), d_att)
        d_proj = jnp.concatenate([d_query, pair_grads], axis=1).astype(bf16)
        d_normed = jnp.einsum("te,de->td", d_proj, wqkv, preferred_element_type=f32)
        d_input, g_gain_one, g_bias_one = jax.vjp(
            layer_norm, layer_input.astype(f32), gains[0], biases[0]
        )[1](d_normed)
        sent = (d_residual + d_input).astype(bf16)
        g_qkv = jnp.einsum("td,te->de", normed, d_proj, preferred_element_type=f32)
        g_out = jnp.einsum("td,te->de", attended, branch_grad, preferred_element_type=f32)
        g_fc = jnp.einsum("td,tf->df", second, d_pre, preferred_element_type=f32)
        g_proj = jnp.einsum("tf,td->fd", activated, mlp_grad, preferred_element_type=f32)
        partial_terms = (
            g_qkv,
            g_out,
            g_fc,
            g_proj,
            jnp.stack([g_gain_one, g_gain_two]),
            jnp.stack([g_bias_one, g_bias_two]),
        )
        running_total = tuple(
            (
                present_value + jnp.where(live_slot, partial_term, 0.0)
                for present_value, partial_term in zip(running_total, partial_terms)
            )
        )
        grad_outputs = store_slot((grad_outputs,), (sent,), slot, live_slot)[0]
        return (sent, grad_outputs, running_total)

    running_init = (
        jnp.zeros((hidden_width, 3 * hidden_width), f32),
        jnp.zeros((hidden_width, hidden_width), f32),
        jnp.zeros((hidden_width, ff_width), f32),
        jnp.zeros((ff_width, hidden_width), f32),
        jnp.zeros((2, hidden_width), f32),
        jnp.zeros((2, hidden_width), f32),
    )
    backward_state = (
        jnp.zeros((tokens, hidden_width), bf16),
        jnp.zeros((micro_count, tokens, hidden_width), bf16),
        running_init,
    )
    ignored, grad_outputs, running_total = lax.fori_loop(
        0, micro_count + 1, backward_tick, backward_state
    )
    shards = (
        lax.psum_scatter(
            running_total[0].astype(jnp.bfloat16), "dp", scatter_dimension=0, tiled=True
        ).astype(jnp.float32),
        lax.psum_scatter(
            running_total[1].astype(jnp.bfloat16), "dp", scatter_dimension=0, tiled=True
        ).astype(jnp.float32),
        lax.psum_scatter(
            running_total[2].astype(jnp.bfloat16), "dp", scatter_dimension=0, tiled=True
        ).astype(jnp.float32),
        lax.psum_scatter(
            running_total[3].astype(jnp.bfloat16), "dp", scatter_dimension=0, tiled=True
        ).astype(jnp.float32),
        lax.psum_scatter(
            running_total[4].astype(jnp.bfloat16), "dp", scatter_dimension=1, tiled=True
        ).astype(jnp.float32),
        lax.psum_scatter(
            running_total[5].astype(jnp.bfloat16), "dp", scatter_dimension=1, tiled=True
        ).astype(jnp.float32),
    )
    g_qkv, g_out, g_fc, g_proj, g_gains, g_biases = (
        lax.psum(shards[0].astype(jnp.bfloat16), "seq").astype(jnp.float32),
        lax.psum(shards[1].astype(jnp.bfloat16), "seq").astype(jnp.float32),
        lax.psum(shards[2].astype(jnp.bfloat16), "seq").astype(jnp.float32),
        lax.psum(shards[3].astype(jnp.bfloat16), "seq").astype(jnp.float32),
        lax.psum(shards[4].astype(jnp.bfloat16), "seq").astype(jnp.float32),
        lax.psum(shards[5].astype(jnp.bfloat16), "seq").astype(jnp.float32),
    )
    return (
        layer_results[None, :, None],
        grad_outputs[None, :, None],
        g_qkv[None],
        g_out[None],
        g_fc[None],
        g_proj[None],
        g_gains[None],
        g_biases[None],
    )


def solution(mesh):
    return jax.shard_map(
        on_device,
        mesh=mesh,
        in_specs=(
            P(None, "dp", "seq", None),
            P(None, "dp", "seq", None),
            P(None, "dp"),
            P(),
            P("section", "dp", None),
            P("section", "dp", None),
            P("section", "dp", None),
            P("section", "dp", None),
            P("section", None, None),
            P("section", None, None),
        ),
        out_specs=(
            P("section", None, "dp", "seq", None),
            P("section", None, "dp", "seq", None),
            P("section", "dp", None),
            P("section", "dp", None),
            P("section", "dp", None),
            P("section", "dp", None),
            P("section", None, "dp"),
            P("section", None, "dp"),
        ),
        check_vma=False,
    )
```

profile of v0, /device:TPU:0, one launch (start us, length us, event | category | flops | bytes accessed | tf_op | source)
XLA Modules:
  0.0 2495.0 jit_solution(6693365417850281291)
XLA Ops:
  22.5 30.0 %all-gather.13.cloned.1.call-done = bf16[1,1120,1120]{2,1,0:T(8,128)(2,1)} async-done(((bf16[1,280,1120]{2,1,0:T(8,128)(2,1)}), bf16[1,1120,1120]{2,1,0:T(8,128)(2,1)}) %all-gather.13.cloned.1.call-update) | async-done | bytes 2508816 | tf_op jit(solution)/shard_map/all_gather | solution.py:67
  52.5 84.1 %all-gather.11.cloned.1.call-done = bf16[1,1120,3360]{2,1,0:T(8,128)(2,1)} async-done(((bf16[1,280,3360]{2,1,0:T(8,128)(2,1)}), bf16[1,1120,3360]{2,1,0:T(8,128)(2,1)}) %all-gather.11.cloned.1.call-update) | async-done | bytes 7526416 | tf_op jit(solution)/shard_map/all_gather | solution.py:66
  136.6 103.8 %all-gather.15.cloned.1.call-done = bf16[1,1120,4480]{2,1,0:T(8,128)(2,1)} async-done(((bf16[1,280,4480]{2,1,0:T(8,128)(2,1)}), bf16[1,1120,4480]{2,1,0:T(8,128)(2,1)}) %all-gather.15.cloned.1.call-update) | async-done | bytes 10035216 | tf_op jit(solution)/shard_map/all_gather | solution.py:68
  240.3 106.0 %all-gather.17.cloned.1.call-done = bf16[1,4480,1120]{2,1,0:T(8,128)(2,1)} async-done(((bf16[1,1120,1120]{2,1,0:T(8,128)(2,1)}), bf16[1,4480,1120]{2,1,0:T(8,128)(2,1)}) %all-gather.17.cloned.1.call-update) | async-done | bytes 10035216 | tf_op jit(solution)/shard_map/all_gather | solution.py:69
  360.4 529.7 %while.116 = (s32[]{:T(128)}, bf16[256,1120]{0,1:T(8,128)(2,1)S(1)}, bf16[2,256,1120]{1,2,0:T(8,128)(2,1)}, bf16[2,256,1120]{1,2,0:T(8,128)(2,1)}, bf16[2,256,11...) while((s32[]{:T(128)}, bf16[256,1120]{0,1:T(8,128)(2,1)S(1)}, ...), condition=%wide.region_8.9_spmd.clone, body=%wide.region_1.8_spmd.clone.sunk | while | flops 9036344320 | bytes 449448800 | solution.py:156
  397.3 68.0 %all-gather.19.cloned.1.call-done = bf16[1024,2240]{0,1:T(8,128)(2,1)} async-done(((bf16[256,2240]{0,1:T(8,128)(2,1)}), bf16[1024,2240]{0,1:T(8,128)(2,1)}) %all-gather.19.cloned.1.call-update) | async-done | bytes 4587536 | tf_op jit(solution)/shard_map/while/body/eval_jaxpr/all_gather | solution.py:92
  482.3 10.7 fusion.219
  497.8 18.4 bitcast_dynamic-update-slice_fusion.21
  522.9 9.5 bitcast_dynamic-update-slice_fusion.22
  569.3 66.2 %all-gather.19.cloned.1.call-done = bf16[1024,2240]{0,1:T(8,128)(2,1)} async-done(((bf16[256,2240]{0,1:T(8,128)(2,1)}), bf16[1024,2240]{0,1:T(8,128)(2,1)}) %all-gather.19.cloned.1.call-update) | async-done | bytes 4587536 | tf_op jit(solution)/shard_map/while/body/eval_jaxpr/all_gather | solution.py:92
  652.6 10.7 fusion.219
  668.0 18.4 bitcast_dynamic-update-slice_fusion.21
  693.1 9.5 bitcast_dynamic-update-slice_fusion.22
  739.5 66.2 %all-gather.19.cloned.1.call-done = bf16[1024,2240]{0,1:T(8,128)(2,1)} async-done(((bf16[256,2240]{0,1:T(8,128)(2,1)}), bf16[1024,2240]{0,1:T(8,128)(2,1)}) %all-gather.19.cloned.1.call-update) | async-done | bytes 4587536 | tf_op jit(solution)/shard_map/while/body/eval_jaxpr/all_gather | solution.py:92
  822.8 10.7 fusion.219
  838.2 18.4 bitcast_dynamic-update-slice_fusion.21
  863.3 9.5 bitcast_dynamic-update-slice_fusion.22
  891.2 866.4 %while.118 = (s32[]{:T(128)}, bf16[256,1120]{0,1:T(8,128)(2,1)}, bf16[2,256,1120]{1,2,0:T(8,128)(2,1)}, f32[1120,3360]{1,0:T(8,128)}, f32[1120,1120]{1,0:T(8,128...) while((s32[]{:T(128)}, bf16[256,1120]{0,1:T(8,128)(2,1)}, ...), condition=%wide.region_26.27_spmd.clone, body=%wide.region_9.26_spmd.clone.sunk | while | flops 17120643072 | bytes 460625856 | solution.py:275
  901.1 16.7 fusion.241
  925.3 57.4 %all-gather.21.cloned.1.call-done = bf16[1024,2240]{0,1:T(8,128)(2,1)} async-done(((bf16[256,2240]{0,1:T(8,128)(2,1)}), bf16[1024,2240]{0,1:T(8,128)(2,1)}) %all-gather.21.cloned.1.call-update) | async-done | bytes 4587536 | tf_op jit(solution)/shard_map/while/body/eval_jaxpr/all_gather | solution.py:233
  987.6 76.9 %while.119 = (s32[]{:T(128)}, bf16[5,4,256,56]{2,3,1,0:T(8,128)(2,1)}, bf16[5,4,256,1024]{3,2,1,0:T(8,128)(2,1)}, bf16[5,4,256,1024]{3,2,1,0:T(8,128)(2,1)}, bf1...) while((s32[]{:T(128)}, ...), condition=%wide.region_16.16_spmd.clone, body=%wide.region_14.15_spmd.clone.sunk | while | flops 368576512 | bytes 36468364 | solution.py:179
  1084.0 10.3 fusion.250
  1102.6 55.1 %reduce-scatter.25.cloned.1.call-done = bf16[256,2240]{0,1:T(8,128)(2,1)} async-done(((bf16[1024,2240]{0,1:T(8,128)(2,1)}), bf16[256,2240]{0,1:T(8,128)(2,1)}) %reduce-scatter.25.cloned.1.call-update) | async-done | bytes 1146896 | tf_op jit(solution)/shard_map/while/body/eval_jaxpr/reduce_scatter | solution.py:194
  1186.2 16.1 fusion.241
  1209.8 60.3 %all-gather.21.cloned.1.call-done = bf16[1024,2240]{0,1:T(8,128)(2,1)} async-done(((bf16[256,2240]{0,1:T(8,128)(2,1)}), bf16[1024,2240]{0,1:T(8,128)(2,1)}) %all-gather.21.cloned.1.call-update) | async-done | bytes 4587536 | tf_op jit(solution)/shard_map/while/body/eval_jaxpr/all_gather | solution.py:233
  1275.1 76.9 %while.119 = (s32[]{:T(128)}, bf16[5,4,256,56]{2,3,1,0:T(8,128)(2,1)}, bf16[5,4,256,1024]{3,2,1,0:T(8,128)(2,1)}, bf16[5,4,256,1024]{3,2,1,0:T(8,128)(2,1)}, bf1...) while((s32[]{:T(128)}, ...), condition=%wide.region_16.16_spmd.clone, body=%wide.region_14.15_spmd.clone.sunk | while | flops 368576512 | bytes 36468364 | solution.py:179
  1373.8 14.4 fusion.250
  1388.2 12.9 fusion.249
  1401.1 44.1 %reduce-scatter.25.cloned.1.call-done = bf16[256,2240]{0,1:T(8,128)(2,1)} async-done(((bf16[1024,2240]{0,1:T(8,128)(2,1)}), bf16[256,2240]{0,1:T(8,128)(2,1)}) %reduce-scatter.25.cloned.1.call-update) | async-done | bytes 1146896 | tf_op jit(solution)/shard_map/while/body/eval_jaxpr/reduce_scatter | solution.py:194
  1456.0 10.3 fusion.247
  1477.3 16.1 fusion.241
  1500.9 60.3 %all-gather.21.cloned.1.call-done = bf16[1024,2240]{0,1:T(8,128)(2,1)} async-done(((bf16[256,2240]{0,1:T(8,128)(2,1)}), bf16[1024,2240]{0,1:T(8,128)(2,1)}) %all-gather.21.cloned.1.call-update) | async-done | bytes 4587536 | tf_op jit(solution)/shard_map/while/body/eval_jaxpr/all_gather | solution.py:233
  1566.2 76.9 %while.119 = (s32[]{:T(128)}, bf16[5,4,256,56]{2,3,1,0:T(8,128)(2,1)}, bf16[5,4,256,1024]{3,2,1,0:T(8,128)(2,1)}, bf16[5,4,256,1024]{3,2,1,0:T(8,128)(2,1)}, bf1...) while((s32[]{:T(128)}, ...), condition=%wide.region_16.16_spmd.clone, body=%wide.region_14.15_spmd.clone.sunk | while | flops 368576512 | bytes 36468364 | solution.py:179
  1664.9 14.4 fusion.250
  1679.3 12.9 fusion.249
  1692.2 44.1 %reduce-scatter.25.cloned.1.call-done = bf16[256,2240]{0,1:T(8,128)(2,1)} async-done(((bf16[1024,2240]{0,1:T(8,128)(2,1)}), bf16[256,2240]{0,1:T(8,128)(2,1)}) %reduce-scatter.25.cloned.1.call-update) | async-done | bytes 1146896 | tf_op jit(solution)/shard_map/while/body/eval_jaxpr/reduce_scatter | solution.py:194
  1747.0 10.3 fusion.247
  1757.6 11.7 convert_element_type.251
  1769.3 14.2 copy.38
  1787.8 10.1 convert_element_type.248
  1798.0 12.4 convert_element_type.250
  1810.5 76.4 %reduce-scatter.17.cloned.1.call-done = bf16[1120,1120]{1,0:T(8,128)(2,1)} async-done(((bf16[4480,1120]{1,0:T(8,128)(2,1)}), bf16[1120,1120]{1,0:T(8,128)(2,1)}) %reduce-scatter.17.cloned.1.call-update) | async-done | bytes 2508816
  1892.1 38.1 %reduce-scatter.21.cloned.1.call-done = bf16[280,1120]{1,0:T(8,128)(2,1)} async-done(((bf16[1120,1120]{1,0:T(8,128)(2,1)}), bf16[280,1120]{1,0:T(8,128)(2,1)}) %reduce-scatter.21.cloned.1.call-update) | async-done | bytes 627216
  1930.2 86.1 %reduce-scatter.19.cloned.1.call-done = bf16[280,3360]{1,0:T(8,128)(2,1)} async-done(((bf16[1120,3360]{1,0:T(8,128)(2,1)}), bf16[280,3360]{1,0:T(8,128)(2,1)}) %reduce-scatter.19.cloned.1.call-update) | async-done | bytes 1881616
  2016.4 187.7 %reduce-scatter.23.cloned.1.call-done = bf16[280,4480]{1,0:T(8,128)(2,1)} async-done(((bf16[1120,4480]{1,0:T(8,128)(2,1)}), bf16[280,4480]{1,0:T(8,128)(2,1)}) %reduce-scatter.23.cloned.1.call-update) | async-done | bytes 2508816
  2205.3 9.3 all-reduce.7
  2214.7 14.9 all-reduce.5
  2230.8 245.7 %all-reduce.10.cloned.1.call-done = (bf16[1,1120,1120]{1,2,0:T(8,128)(2,1)}, bf16[1,280,3360]{2,1,0:T(8,128)(2,1)}, bf16[1,280,1120]{2,1,0:T(8,128)(2,1)}, bf16[1,280,4480]{2,1,0:T(8,128)(2,1)}) async-done(((bf16[1,1120,1120]{1,2,0:T(8,128)(2,1)}, bf16[1,280,3360]{2,1,0:T(8,128)(2,1)}, bf16[1,280,1120]{2,1,0:T(8,128)(2,1)}, bf16[1,280,4480]{2,1,0:T(8,128)(2,1)}), (bf16[1,1120,1120]{1,2,0:T(8,128)(2,1)}, ...) | async-done | bytes 7526416 | tf_op jit(solution)/shard_map/psum | solution.py:302
  (779 shorter events, 656.8 us)
Async XLA Ops:
  7.2 45.3 %all-gather.13.cloned.1.call-start = ((), (), s32[]{:S(2)}) async-start(), calls=%async_computation.6 | async-start | bytes 3225600 | tf_op jit(solution)/shard_map/all_gather | solution.py:67
  9.4 127.1 %all-gather.11.cloned.1.call-start = ((), (), s32[]{:S(2)}) async-start(), calls=%async_computation.5 | async-start | bytes 9676800 | tf_op jit(solution)/shard_map/all_gather | solution.py:66
  13.1 227.3 %all-gather.15.cloned.1.call-start = ((), (), s32[]{:S(2)}) async-start(), calls=%async_computation.7 | async-start | bytes 12544000 | tf_op jit(solution)/shard_map/all_gather | solution.py:68
  17.3 329.0 %all-gather.17.cloned.1.call-start = ((), (), s32[]{:S(2)}) async-start(), calls=%async_computation.8 | async-start | bytes 12902400 | tf_op jit(solution)/shard_map/all_gather | solution.py:69
  360.5 104.7 %all-gather.19.cloned.1.call-start = ((), (), s32[]{:S(2)}) async-start(), calls=%async_computation.14 | async-start | bytes 5734400 | tf_op jit(solution)/shard_map/while/body/eval_jaxpr/all_gather | solution.py:92
  361.4 4.7 collective-permute-start
  496.8 21.6 slice-start.3
  496.8 21.6 slice-start.8
  532.4 103.0 %all-gather.19.cloned.1.call-start = ((), (), s32[]{:S(2)}) async-start(), calls=%async_computation.14 | async-start | bytes 5734400 | tf_op jit(solution)/shard_map/while/body/eval_jaxpr/all_gather | solution.py:92
  533.3 4.8 collective-permute-start
  667.0 21.7 slice-start.3
  667.0 21.7 slice-start.8
  668.0 20.7 slice-start.4
  668.0 20.7 slice-start.9
  668.0 20.7 slice-start.10
  702.7 103.0 %all-gather.19.cloned.1.call-start = ((), (), s32[]{:S(2)}) async-start(), calls=%async_computation.14 | async-start | bytes 5734400 | tf_op jit(solution)/shard_map/while/body/eval_jaxpr/all_gather | solution.py:92
  703.5 4.8 collective-permute-start
  837.2 21.7 slice-start.3
  837.2 21.7 slice-start.8
  838.2 20.7 slice-start.4
  838.2 20.7 slice-start.9
  838.2 20.7 slice-start.10
  891.2 91.5 %all-gather.21.cloned.1.call-start = ((), (), s32[]{:S(2)}) async-start(), calls=%async_computation.15 | async-start | bytes 5734400 | tf_op jit(solution)/shard_map/while/body/eval_jaxpr/all_gather | solution.py:233
  891.3 8.5 collective-permute-start.1
  896.5 261.2 %reduce-scatter.25.cloned.1.call-start = ((), (), s32[]{:S(2)}) async-start(), calls=%async_computation.16 | async-start | bytes 5734400 | tf_op jit(solution)/shard_map/while/body/eval_jaxpr/reduce_scatter | solution.py:194
  925.3 62.4 %slice-start.5 = ((bf16[256,3360]{0,1:T(8,128)(2,1)}), bf16[256,1120]{0,1:T(8,128)(2,1)S(1)}, s32[]{:S(2)}) async-start(bf16[256,3360]{0,1:T(8,128)(2,1)} %copy-done.3), calls=%async_computation.22 | async-start | bytes 1146880 | tf_op jit(solution)/shard_map/while/body/eval_jaxpr/slice | solution.py:159
  1094.3 63.4 %copy-start.21 = (bf16[5,4,256,56]{2,3,1,0:T(8,128)(2,1)S(1)}, bf16[5,4,256,56]{2,3,1,0:T(8,128)(2,1)}, u32[]{:S(2)}) copy-start(bf16[5,4,256,56]{2,3,1,0:T(8,128)(2,1)} %get-tuple-element.2242) | copy-start | bytes 1720324 | tf_op jit(solution)/shard_map/while
  1094.3 63.4 %copy-start.29 = (f32[1120]{0:T(1024)S(1)}, f32[1120]{0:T(1024)}, u32[]{:S(2)}) copy-start(f32[1120]{0:T(1024)} %get-tuple-element.2234) | copy-start | bytes 13444 | tf_op jit(solution)/shard_map/while
  1175.3 94.9 %all-gather.21.cloned.1.call-start = ((), (), s32[]{:S(2)}) async-start(), calls=%async_computation.15 | async-start | bytes 5734400 | tf_op jit(solution)/shard_map/while/body/eval_jaxpr/all_gather | solution.py:233
  1176.5 8.5 collective-permute-start.1
  1181.7 263.6 %reduce-scatter.25.cloned.1.call-start = ((), (), s32[]{:S(2)}) async-start(), calls=%async_computation.16 | async-start | bytes 5734400 | tf_op jit(solution)/shard_map/while/body/eval_jaxpr/reduce_scatter | solution.py:194
  1209.8 65.3 %slice-start.5 = ((bf16[256,3360]{0,1:T(8,128)(2,1)}), bf16[256,1120]{0,1:T(8,128)(2,1)S(1)}, s32[]{:S(2)}) async-start(bf16[256,3360]{0,1:T(8,128)(2,1)} %copy-done.3), calls=%async_computation.22 | async-start | bytes 1146880 | tf_op jit(solution)/shard_map/while/body/eval_jaxpr/slice | solution.py:159
  1388.2 57.0 %copy-start.21 = (bf16[5,4,256,56]{2,3,1,0:T(8,128)(2,1)S(1)}, bf16[5,4,256,56]{2,3,1,0:T(8,128)(2,1)}, u32[]{:S(2)}) copy-start(bf16[5,4,256,56]{2,3,1,0:T(8,128)(2,1)} %get-tuple-element.2242) | copy-start | bytes 1720324 | tf_op jit(solution)/shard_map/while
  1388.2 57.0 %copy-start.29 = (f32[1120]{0:T(1024)S(1)}, f32[1120]{0:T(1024)}, u32[]{:S(2)}) copy-start(f32[1120]{0:T(1024)} %get-tuple-element.2234) | copy-start | bytes 13444 | tf_op jit(solution)/shard_map/while
  1466.3 94.9 %all-gather.21.cloned.1.call-start = ((), (), s32[]{:S(2)}) async-start(), calls=%async_computation.15 | async-start | bytes 5734400 | tf_op jit(solution)/shard_map/while/body/eval_jaxpr/all_gather | solution.py:233
  1467.5 8.5 collective-permute-start.1
  1472.7 263.6 %reduce-scatter.25.cloned.1.call-start = ((), (), s32[]{:S(2)}) async-start(), calls=%async_computation.16 | async-start | bytes 5734400 | tf_op jit(solution)/shard_map/while/body/eval_jaxpr/reduce_scatter | solution.py:194
  1500.9 65.3 %slice-start.5 = ((bf16[256,3360]{0,1:T(8,128)(2,1)}), bf16[256,1120]{0,1:T(8,128)(2,1)S(1)}, s32[]{:S(2)}) async-start(bf16[256,3360]{0,1:T(8,128)(2,1)} %copy-done.3), calls=%async_computation.22 | async-start | bytes 1146880 | tf_op jit(solution)/shard_map/while/body/eval_jaxpr/slice | solution.py:159
  1679.3 57.0 %copy-start.21 = (bf16[5,4,256,56]{2,3,1,0:T(8,128)(2,1)S(1)}, bf16[5,4,256,56]{2,3,1,0:T(8,128)(2,1)}, u32[]{:S(2)}) copy-start(bf16[5,4,256,56]{2,3,1,0:T(8,128)(2,1)} %get-tuple-element.2242) | copy-start | bytes 1720324 | tf_op jit(solution)/shard_map/while
  1679.3 57.0 %copy-start.29 = (f32[1120]{0:T(1024)S(1)}, f32[1120]{0:T(1024)}, u32[]{:S(2)}) copy-start(f32[1120]{0:T(1024)} %get-tuple-element.2234) | copy-start | bytes 13444 | tf_op jit(solution)/shard_map/while
  1757.5 129.4 %reduce-scatter.17.cloned.1.call-start = ((), (), s32[]{:S(2)}) async-start(), calls=%async_computation.9 | async-start | bytes 12902400
  1783.5 146.7 %reduce-scatter.21.cloned.1.call-start = ((), (), s32[]{:S(2)}) async-start(), calls=%async_computation.11 | async-start | bytes 3225600
  1787.8 228.6 %reduce-scatter.19.cloned.1.call-start = ((), (), s32[]{:S(2)}) async-start(), calls=%async_computation.10 | async-start | bytes 9676800
  1797.9 406.1 %reduce-scatter.23.cloned.1.call-start = ((), (), s32[]{:S(2)}) async-start(), calls=%async_computation.12 | async-start | bytes 12544000
  1810.4 666.0 %all-reduce.10.cloned.1.call-start = ((), (), s32[]{:S(2)}) async-start(), calls=%async_computation.13 | async-start | bytes 15339520 | tf_op jit(solution)/shard_map/psum | solution.py:302
  1892.1 312.0 %copy-start.49 = (u32[32]{0:T(128)S(1)}, u32[32]{0:T(128)}, u32[]{:S(2)}) copy-start(u32[32]{0:T(128)} %constant.840) | copy-start | bytes 388
  1892.1 313.2 %copy-start.38 = (f32[2,1120]{1,0:T(2,128)S(1)}, f32[2,1120]{1,0:T(2,128)}, u32[]{:S(2)}) copy-start(f32[2,1120]{1,0:T(2,128)} %get-tuple-element.1197) | copy-start | bytes 26884
  1892.1 313.2 %copy-start.41 = (f32[2,1120]{1,0:T(2,128)S(1)}, f32[2,1120]{1,0:T(2,128)}, u32[]{:S(2)}) copy-start(f32[2,1120]{1,0:T(2,128)} %get-tuple-element.1198) | copy-start | bytes 26884
  (150 other events, 1133.4 us)
Sparse Core Ops, SparseCore 0:
  10.4 41.9 all-gather.12
  54.3 82.2 all-gather.10
  139.0 101.3 all-gather.14
  242.6 103.6 all-gather.16
  378.2 86.9 all-gather.18
  550.2 85.2 all-gather.18
  720.4 85.2 all-gather.18
  896.6 85.9 all-gather.20
  1076.4 81.2 reduce-scatter.24
  1181.8 88.3 all-gather.20
  1363.9 81.2 reduce-scatter.24
  1472.8 88.3 all-gather.20
  1655.0 81.2 reduce-scatter.24
  1783.6 103.2 reduce-scatter.16
  1890.7 39.5 reduce-scatter.20
  1933.2 83.1 reduce-scatter.18
  2018.7 185.2 reduce-scatter.22
  2207.3 269.1 all-reduce.9
where the time goes:
time: 2500 us
  waiting for transfers between devices  1480 us (59%)
  matrix products  511 us (20%)
  other arithmetic  250 us (10%)
  local copies, waits for them, and re-layouts  183 us (7%)
    unnamed x13, waiting for transfers between devices  388 us
    psum x1, waiting for transfers between devices, on_device(): lax.psum(shards[3].astype(jnp.bfloat16), 'seq').astype(jnp.float32)  246 us
    all_gather x3, waiting for transfers between devices, forward(): lax.all_gather(projected[:, hidden_width:], 'seq', axis=0, tiled=True)  200 us
    all_gather x3, waiting for transfers between devices, backward_tick(): lax.all_gather(projected[:, hidden_width:], 'seq', axis=0, tiled=True)  178 us
    reduce_scatter x3, waiting for transfers between devices, attention_back(): lax.psum_scatter(jnp.concatenate([d_key, d_value], axis=1).astype(jnp.bfl...  143 us
    all_gather x1, waiting for transfers between devices, on_device(): lax.all_gather(w_proj[0].astype(bf16), 'dp', axis=0, tiled=True)  106 us
    sub x15, other arithmetic, one_group(): d_prob - row_inner[..., None]  105 us
    all_gather x1, waiting for transfers between devices, on_device(): lax.all_gather(w_fc[0].astype(bf16), 'dp', axis=0, tiled=True)  104 us
  transfers between devices with their start and end apart: 24, of which 18 were waited for; matrix products, arithmetic and copies ran while one was open for 12% of the time, Pallas kernels for 0%

commit v1 on v0

v1 whole, which is shorter than its diff:
```python
import functools
import math

import jax
import jax.numpy as jnp
from jax import lax
from jax.experimental import pallas as pl
from jax.experimental.pallas import tpu as pltpu
from jax.sharding import PartitionSpec as P

HEADS = 20
HEAD_DIM = 56
EPS = 1e-05
NEG = -1e30
LANES = 128
WINDOW = 256
VMEM_LIMIT = 58 * 1024 * 1024
MESH = pl.DeviceIdType.MESH

bf16 = jnp.bfloat16
f32 = jnp.float32


def round_up(size, grain):
    return -(-size // grain) * grain


def dot_nn(left, right):
    return lax.dot_general(left, right, (((1,), (0,)), ((), ())), preferred_element_type=f32)


def dot_nt(left, right):
    return lax.dot_general(left, right, (((1,), (1,)), ((), ())), preferred_element_type=f32)


def dot_tn(left, right):
    return lax.dot_general(left, right, (((0,), (0,)), ((), ())), preferred_element_type=f32)


LINKED = 4


def greet(*places):
    barrier = pltpu.get_barrier_semaphore()
    for place in places:
        pl.semaphore_signal(barrier, inc=1, device_id=place, device_id_type=MESH)
    pl.semaphore_wait(barrier, len(places))


def remote_copy(source, target, send, recv, **place):
    return pltpu.make_async_remote_copy(
        src_ref=source, dst_ref=target, send_sem=send, recv_sem=recv, device_id=place, device_id_type=MESH
    )


def pair_places():
    z = lax.axis_index("seq")
    return {"seq": z + 1 - 2 * lax.rem(z, 2)}, {"section": 1 - lax.axis_index("section")}


def partners():
    core = lax.axis_index("section")
    rank = lax.axis_index("dp")
    x, y = lax.rem(rank, 2), rank // 2
    near = lax.rem(y + core, 2) * 2 + lax.rem(x + 1 - core, 2)
    far = lax.rem(y + 1 - core, 2) * 2 + lax.rem(x + core, 2)
    return near, far, 3 - rank


def vmem_specs(count):
    return [pl.BlockSpec(memory_space=pltpu.VMEM)] * count


def any_specs(count):
    return [pl.BlockSpec(memory_space=pl.ANY)] * count


def sum_of(parts):
    return functools.reduce(jnp.add, parts)


def load_all(copies):
    for copy in copies:
        copy.start()


class Reduction:
    def __init__(self, arrays, parts):
        self.arrays = [(a.shape, a.dtype) for a in arrays]
        self.chunks = []
        for index, (shape, _) in enumerate(self.arrays):
            step = round_up(-(-shape[1] // parts[index]), 16)
            self.chunks += [(index, a, min(step, shape[1] - a)) for a in range(0, shape[1], step)]
        self.count = len(self.chunks)
        self.classes, self.places = {}, []
        for array, _, rows in self.chunks:
            (_, _, columns), dtype = self.arrays[array]
            key = (columns > 2048, str(dtype))
            most = self.classes.setdefault(key, [0, 0, 0, dtype])
            self.places.append((list(self.classes).index(key), most[0]))
            most[:3] = [most[0] + 1, max(most[1], rows), max(most[2], columns)]

    def out_shapes(self):
        return tuple(jax.ShapeDtypeStruct(shape[1:], dtype) for shape, dtype in self.arrays)

    def scratch(self):
        sizes = [((rows, self.arrays[a][0][2]), self.arrays[a][1]) for a, _, rows in self.chunks]
        many = [pltpu.VMEM((4,) + s, t) for s, t in sizes] + [pltpu.VMEM((2,) + s, t) for s, t in sizes]
        single = [pltpu.VMEM(s, t) for s, t in sizes] * 3
        slots = [pltpu.VMEM((4,) + tuple(c[1:3]), c[3]) for c in self.classes.values() for _ in range(2)]
        n = self.count
        dma = pltpu.SemaphoreType.DMA
        sems = [dma((n, 4)), dma((n, 4)), dma((n, 4)), dma((n, 3)), dma((n, 3)), dma((n, 3)), dma((n, 3))]
        return many + single + slots + sems + [pltpu.SemaphoreType.REGULAR((len(self.classes),))]

    def bind(self, kept, given, results, scratch):
        n, k = self.count, len(self.classes)
        self.kept, self.given, self.results = kept, given, results
        self.here, self.came, self.far_in, self.z_in, self.z_mid = (scratch[i * n:(i + 1) * n] for i in range(5))
        self.slots, rest = scratch[5 * n:5 * n + 2 * k], scratch[5 * n + 2 * k:]
        (self.load_sem, self.core_send, self.core_recv, self.dp_send, self.dp_recv, self.z_send, self.z_recv, self.free) = rest
        z = lax.axis_index("seq")
        self.rank = lax.axis_index("dp")
        self.near, self.far, self.across = partners()
        self.inner = (z == 1) | (z == 2)
        self.pair_z, self.other_z = z + 1 - 2 * lax.rem(z, 2), 3 - z
        self.other_core = {"section": 1 - lax.axis_index("section")}
        self.settled = lambda chunk: None

    def peers(self):
        return [{"dp": self.near}, {"dp": self.far}, {"seq": self.pair_z}, {"seq": self.other_z}, self.other_core]

    def loads(self, c):
        array, row, rows = self.chunks[c]
        return [
            pltpu.make_async_copy(
                self.kept[array].at[block, pl.ds(row, rows)], self.here[c].at[i], self.load_sem.at[c, i]
            )
            for i, block in enumerate((self.near, self.across, self.far, self.rank))
        ]

    def slot(self, c, index):
        array, _, rows = self.chunks[c]
        kind, at = self.places[c]
        return self.slots[2 * kind + at % 2].at[index, pl.ds(0, rows), pl.ds(0, self.arrays[array][0][2])]

    def to_core(self, c):
        array, row, rows = self.chunks[c]
        return [
            remote_copy(
                self.given[array].at[block, pl.ds(row, rows)],
                self.slot(c, i),
                self.core_send.at[c, i],
                self.core_recv.at[c, i],
                **self.other_core,
            )
            for i, block in enumerate((self.far, self.across, self.near, self.rank))
        ]

    def nears(self, c):
        return [
            remote_copy(self.here[c].at[i], self.came[c].at[i], self.dp_send.at[c, i], self.dp_recv.at[c, i], dp=self.near)
            for i in range(2)
        ]

    def fars(self, c):
        return remote_copy(self.here[c].at[2], self.far_in[c], self.dp_send.at[c, 2], self.dp_recv.at[c, 2], dp=self.far)

    def along(self, c, k):
        source = self.z_mid[c] if k == 2 else self.here[c].at[3]
        target = self.z_mid[c] if k == 1 else self.z_in[c]
        place = self.other_z if k == 1 else self.pair_z
        return remote_copy(source, target, self.z_send.at[c, k], self.z_recv.at[c, k], seq=place)

    def add(self, c, index, *others):
        here = self.here[c]
        total = here[index].astype(f32)
        for other in others:
            total = total + other[...].astype(f32)
        here[index] = total.astype(here.dtype)

    def store(self, c, value):
        array, row, rows = self.chunks[c]
        self.results[array][pl.ds(row, rows)] = value
        self.settled(c)

    def open(self):
        for c in range(self.count):
            load_all(self.loads(c))

    def give(self, c=0):
        kind, at = self.places[c]
        if at >= 2:
            pl.semaphore_wait(self.free.at[kind], 1)
        load_all(self.to_core(c))

    def begin(self, c):
        for copy in self.loads(c):
            copy.wait()
        for copy in self.to_core(c):
            copy.wait_recv()
        for i in range(2):
            self.add(c, i, self.slot(c, i))
        load_all(self.nears(c))
        for i in (2, 3):
            self.add(c, i, self.slot(c, i))
        kind, at = self.places[c]
        if (kind, at + 2) in self.places:
            pl.semaphore_signal(self.free.at[kind], inc=1, device_id=self.other_core, device_id_type=MESH)
        if c + 2 < self.count:
            self.give(c + 2)

    def after_near(self, c):
        for copy in self.nears(c):
            copy.wait()
        self.add(c, 2, self.came[c].at[1])
        self.fars(c).start()

    def after_far(self, c):
        self.fars(c).wait()
        self.add(c, 3, self.came[c].at[0], self.far_in[c])
        pl.when(jnp.logical_not(self.inner))(self.along(c, 0).start)

    def after_inward(self, c):
        pl.when(jnp.logical_not(self.inner))(self.along(c, 0).wait_send)

        @pl.when(self.inner)
        def add():
            self.along(c, 0).wait_recv()
            self.add(c, 3, self.z_in[c])
            self.along(c, 1).start()

    def after_middle(self, c):
        @pl.when(self.inner)
        def add():
            self.along(c, 1).wait()
            total = self.here[c][3].astype(f32) + self.z_mid[c][...].astype(f32)
            self.z_mid[c][...] = total.astype(self.z_mid[c].dtype)
            self.along(c, 2).start()
            self.store(c, self.z_mid[c][...])

    def after_outward(self, c):
        pl.when(self.inner)(self.along(c, 2).wait_send)

        @pl.when(jnp.logical_not(self.inner))
        def take():
            self.along(c, 2).wait_recv()
            self.store(c, self.z_in[c][...])

        for copy in self.to_core(c):
            copy.wait_send()

    def turns(self):
        steps = (self.begin, self.after_near, self.after_far, self.after_inward, self.after_middle, self.after_outward)

        def turn(number):
            for lag, step in enumerate(steps):
                if 0 <= number - lag < self.count:
                    step(number - lag)

        return [functools.partial(turn, number) for number in range(self.count + len(steps) - 1)]


class Homes:
    def __init__(self, items):
        self.items = items
        self.count = 1 + max(target for _, target in items)

    def out_shapes(self, rows):
        return (jax.ShapeDtypeStruct((2,) + rows.shape, rows.dtype),) * self.count

    def scratch(self):
        dma = pltpu.SemaphoreType.DMA
        n = len(self.items)
        return [dma((n, 2)), dma((n, 2)), dma((n,))]

    def bind(self, rows, homes, scratch):
        self.rows, self.homes = rows, homes
        self.send, self.recv, self.local = scratch
        z = lax.axis_index("seq")
        self.group = z // 2
        self.swapped = z + 2 - 4 * self.group
        self.first_core = lax.axis_index("section") == 0

    def peers(self):
        return [{"section": section, "seq": self.swapped} for section in range(2)]

    def target(self, i):
        return self.homes[self.items[i][1]].at[self.group]

    def stays(self, i):
        return pltpu.make_async_copy(self.rows[i], self.target(i), self.local.at[i])

    def beside(self, i):
        return remote_copy(self.rows[i], self.target(i), self.send.at[i, 0], self.recv.at[i, 0], section=1)

    def away(self, i):
        layer = self.items[i][0]
        return remote_copy(
            self.rows[i], self.target(i), self.send.at[i, 1], self.recv.at[i, 1], section=layer, seq=self.swapped
        )

    def start(self):
        @pl.when(self.first_core)
        def first():
            for i, (layer, _) in enumerate(self.items):
                (self.stays(i) if layer == 0 else self.beside(i)).start()

        @pl.when(jnp.logical_not(self.first_core))
        def second():
            for i in range(len(self.items)):
                self.away(i).start()

    def finish(self):
        @pl.when(self.first_core)
        def first():
            for i, (layer, _) in enumerate(self.items):
                if layer == 0:
                    self.stays(i).wait()
                    self.away(i).wait_recv()
                else:
                    self.beside(i).wait_send()

        @pl.when(jnp.logical_not(self.first_core))
        def second():
            for i, (layer, _) in enumerate(self.items):
                self.away(i).wait_send()
                if layer == 1:
                    self.beside(i).wait_recv()
                    self.away(i).wait_recv()


HEAD_GROUPS = ((0, 6), (6, 6), (12, 6), (18, 2))
LANES_IN = ((0, 384), (384, 384), (768, 256), (1024, 128))
BACKWARD_ORDER = (
    "p", "t", "p", "t", "p", "s0", "t", "p", "p", "t", "p", "s1", "a0", "t", "p", "p", "t", "p", "s2", "a1",
    "t", "a2", "p", "s3", "t", "a3", "t", "z",
)
LANES_OUT = ((0, 256), (256, 384), (640, 256), (896, 256))


def window_in(group, head):
    return head // 3 if group == 0 else (7 * head - 10) // 16


def window_out(group, head):
    return 7 if group == 3 else 7 * head // 16


def head_window(head, tile, rows):
    start = pl.multiple_of(tile * LANES, LANES)
    lane = lax.broadcasted_iota(jnp.int32, (rows, WINDOW), 1) + (start - head * HEAD_DIM)
    return pl.ds(start, WINDOW), (lane >= 0) & (lane < HEAD_DIM)


def two_heads(group, step, work):
    def pair(i, carry):
        work(group, 2 * i)
        work(group, 2 * i + 1)
        return carry

    lax.fori_loop(step, step + 1, pair, 0)


def heads_of(group, work):
    first, count = HEAD_GROUPS[group]

    def pair(step, carry):
        work(group, first + 2 * step)
        work(group, first + 2 * step + 1)
        return carry

    lax.fori_loop(0, count // 2, pair, 0)


def fill_bias(bias, place, row_axis):
    blocks, tokens, _ = bias.shape
    row = lax.broadcasted_iota(jnp.int32, (tokens, tokens), row_axis) + place[1]
    for b in range(blocks):
        column = lax.broadcasted_iota(jnp.int32, (tokens, tokens), 1 - row_axis) + place[1 + b]
        bias[b] = jnp.where((column <= row) & (column < place[0]), 0.0, NEG)


def attention_steps(place, q_ref, kv_refs, o_pad, lse_ref, bias, links):
    tokens, blocks = q_ref.shape[0], len(kv_refs)
    scale = HEAD_DIM ** -0.5
    groups = range(len(HEAD_GROUPS))

    def copies(group):
        send, recv = links
        along, beside = pair_places()
        lanes = (slice(None), slice(None), pl.ds(*LANES_IN[group]))

        def copy(k, source, target, place):
            return remote_copy(
                kv_refs[source].at[lanes], kv_refs[target].at[lanes], send.at[group, k], recv.at[group, k], **place
            )

        return copy(0, 0, 1, along), copy(1, 0, 2, beside), copy(2, 1, 3, beside)

    def start():
        if links:
            for group in groups:
                copies(group)[0].start()
                copies(group)[1].start()
        o_pad[...] = jnp.zeros(o_pad.shape, o_pad.dtype)
        fill_bias(bias, place, 0)
        lse_ref[...] = jnp.zeros(lse_ref.shape, f32)

    def one_head(group, head):
        lse_lane = lax.broadcasted_iota(jnp.int32, lse_ref.shape, 1)
        lanes, inside = head_window(head, window_in(group, head), tokens)
        query = jnp.where(inside, q_ref[:, lanes], 0).astype(bf16)
        scores = [dot_nt(query, kv_refs[b][0, :, lanes]) * scale + bias[b] for b in range(blocks)]
        peak = jnp.max(functools.reduce(jnp.maximum, scores), axis=1, keepdims=True)
        weights = [jnp.exp(s - peak) for s in scores]
        total = jnp.sum(functools.reduce(jnp.add, weights), axis=1, keepdims=True)
        share = 1.0 / total
        out = sum_of([dot_nn((w * share).astype(bf16), kv_refs[b][1, :, lanes]) for b, w in enumerate(weights)])
        o_pad[:, lanes] = jnp.where(inside, out, o_pad[:, lanes].astype(f32)).astype(bf16)
        lse_ref[...] = jnp.where(lse_lane == head, peak + jnp.log(total), lse_ref[...])

    def work(group):
        if links:
            first, second, third = copies(group)
            first.wait_recv()
            third.start()
            second.wait_recv()
            third.wait_recv()
        heads_of(group, one_head)

    def end():
        if links:
            for group in groups:
                for copy in copies(group):
                    copy.wait_send()

    return start, work, end


def attention_forward_kernel(blocks, place, q_ref, *refs):
    o_ref, lse_ref, bias = refs[blocks:]
    start, work, _ = attention_steps(place, q_ref, refs[:blocks], o_ref, lse_ref, bias, ())
    start()
    for group in range(len(HEAD_GROUPS)):
        work(group)


def attention_forward(place, query, kv_blocks, blocks):
    tokens, width = query.shape
    results = pl.pallas_call(
        functools.partial(attention_forward_kernel, blocks),
        out_shape=(
            jax.ShapeDtypeStruct((tokens, width), bf16),
            jax.ShapeDtypeStruct((tokens, LANES), f32),
        ),
        in_specs=[pl.BlockSpec(memory_space=pltpu.SMEM)] + vmem_specs(1 + len(kv_blocks)),
        out_specs=tuple(vmem_specs(2)),
        scratch_shapes=[pltpu.VMEM((blocks, tokens, tokens), f32)],
        compiler_params=pltpu.CompilerParams(vmem_limit_bytes=VMEM_LIMIT),
        cost_estimate=pl.CostEstimate(
            flops=4 * HEADS * tokens * tokens * blocks * WINDOW,
            bytes_accessed=60_000_000,
            transcendentals=HEADS * tokens * tokens * blocks,
        ),
        name="attention_forward",
    )(place, query, *kv_blocks)
    return results[0], results[1], kv_blocks


def attention_backward_kernel(blocks, reduction, going, place, q_ref, d_ref, lse_ref, *refs):
    kv_refs, refs = refs[:blocks], refs[blocks:]
    turns = []
    linked = reduction is not None
    if linked:
        arrays = len(reduction.arrays)
        kept, given, refs = refs[:arrays], refs[arrays:2 * arrays], refs[2 * arrays:]
        rows, refs = refs[:len(going.items)], refs[len(going.items):]
        dq_ref, out_ref, refs = refs[0], refs[1], refs[2:]
        results, refs = refs[:arrays], refs[arrays:]
        homes, refs = refs[:going.count], refs[going.count:]
        dq_pad, bias, grads, from_core, from_pair, send, recv = refs[:7]
        going.bind(rows, homes, refs[7:10])
        reduction.bind(kept, given, results, refs[10:])
        along, beside = pair_places()
        reduction.open()
        greet(*reduction.peers(), *going.peers())
        reduction.give(0)
        reduction.give(1)
        going.start()
        turns = reduction.turns()
    else:
        dq_ref, refs = refs[0], refs[1:]
        out_refs, (dq_pad, bias, grads) = refs[:blocks], refs[blocks:]
    tokens = q_ref.shape[0]
    scale = HEAD_DIM ** -0.5
    dq_pad[...] = jnp.zeros(dq_pad.shape, dq_pad.dtype)
    for b in range(blocks):
        grads[b] = jnp.zeros(grads.shape[1:], grads.dtype)
    fill_bias(bias, place, 1)

    def one_head(group, head):
        lanes, inside = head_window(head, window_out(group, head), tokens)
        query = jnp.where(inside, q_ref[:, lanes], 0).astype(bf16)
        grad = jnp.where(inside, d_ref[:, lanes], 0).astype(bf16)
        lse = lse_ref[pl.ds(head, 1), :]
        probs = [
            jnp.exp(dot_nt(kv_refs[b][0, :, lanes], query) * scale + bias[b] - lse) for b in range(blocks)
        ]
        d_probs = [dot_nt(kv_refs[b][1, :, lanes], grad) for b in range(blocks)]
        inner = jnp.sum(sum_of([p * dp for p, dp in zip(probs, d_probs)]), axis=0, keepdims=True)
        d_query = None
        for b in range(blocks):
            d_score = (probs[b] * (d_probs[b] - inner) * scale).astype(bf16)
            grads[b, 0, :, lanes] = grads[b, 0, :, lanes] + dot_nn(d_score, query).astype(bf16)
            grads[b, 1, :, lanes] = grads[b, 1, :, lanes] + dot_nn(probs[b].astype(bf16), grad).astype(bf16)
            part = dot_tn(d_score, kv_refs[b][0, :, lanes])
            d_query = part if d_query is None else d_query + part
        dq_pad[:, lanes] = jnp.where(inside, d_query, dq_pad[:, lanes].astype(f32)).astype(bf16)

    def lanes_of(group):
        return (slice(None), slice(None), pl.ds(*LANES_OUT[group]))

    def to_core(group, k):
        lanes = lanes_of(group)
        return remote_copy(
            grads.at[2 + k].at[lanes], from_core.at[k].at[lanes], send.at[group, k], recv.at[group, k], **beside
        )

    def to_pair(group):
        lanes = lanes_of(group)
        return remote_copy(
            grads.at[1].at[lanes], from_pair.at[lanes], send.at[group, 2], recv.at[group, 2], **along
        )

    def add_core(group):
        lanes = lanes_of(group)
        for k in (1, 0):
            to_core(group, k).wait_recv()
            mine = grads.at[k]
            mine[lanes] = (mine[lanes].astype(f32) + from_core.at[k][lanes].astype(f32)).astype(bf16)
            if k == 1:
                to_pair(group).start()

    groups = range(len(HEAD_GROUPS))
    if not linked:
        for group in groups:
            heads_of(group, one_head)
        dq_ref[...] = dq_pad[...]
        for b in range(blocks):
            out_refs[b][...] = grads[b]
        return

    def last_add():
        for group in groups:
            lanes = lanes_of(group)
            to_pair(group).wait_recv()
            out_ref[lanes] = (grads.at[0][lanes].astype(f32) + from_pair[lanes].astype(f32)).astype(bf16)

    heads = [(group, (first + h) // 2) for group, (first, count) in enumerate(HEAD_GROUPS) for h in range(0, count, 2)]
    for step in BACKWARD_ORDER:
        if step == "p":
            two_heads(*heads.pop(0), one_head)
        elif step == "t":
            turns.pop(0)()
        elif step == "z":
            last_add()
        elif step[0] == "s":
            to_core(int(step[1]), 1).start()
            to_core(int(step[1]), 0).start()
        else:
            add_core(int(step[1]))
    for turn in turns:
        turn()
    dq_ref[...] = dq_pad[...]
    for group in groups:
        to_core(group, 0).wait_send()
        to_core(group, 1).wait_send()
        to_pair(group).wait_send()
    going.finish()


def attention_backward(place, query, d_out, lse_rows, kv_blocks, kept=(), given=(), parts=(), layers=(), rows=()):
    blocks = len(kv_blocks)
    tokens, width = query.shape
    one = jax.ShapeDtypeStruct((2, tokens, width), bf16)
    reduction = Reduction(kept, parts) if kept else None
    going = Homes([(layer, 0) for layer in layers]) if kept else None
    own = [one] * (1 if kept else blocks)
    dma = pltpu.SemaphoreType.DMA((len(HEAD_GROUPS), 3))
    linked = []
    if kept:
        linked = [pltpu.VMEM((2, 2, tokens, width), bf16), pltpu.VMEM((2, tokens, width), bf16), dma, dma]
        linked += going.scratch() + reduction.scratch()
    results = pl.pallas_call(
        functools.partial(attention_backward_kernel, blocks, reduction, going),
        out_shape=(jax.ShapeDtypeStruct((tokens, width), bf16),)
        + tuple(own)
        + (reduction.out_shapes() + going.out_shapes(rows[0]) if kept else ()),
        in_specs=[pl.BlockSpec(memory_space=pltpu.SMEM)] + vmem_specs(3 + blocks) + any_specs(2 * len(kept) + len(rows)),
        out_specs=tuple(vmem_specs(1 + len(own) + len(kept)) + any_specs(1 if kept else 0)),
        scratch_shapes=[
            pltpu.VMEM((tokens, width), bf16),
            pltpu.VMEM((blocks, tokens, tokens), f32),
            pltpu.VMEM((blocks, 2, tokens, width), bf16),
        ]
        + linked,
        compiler_params=pltpu.CompilerParams(
            vmem_limit_bytes=VMEM_LIMIT, **(dict(collective_id=4 + len(rows), has_side_effects=True) if kept else {})
        ),
        cost_estimate=pl.CostEstimate(
            flops=10 * HEADS * tokens * tokens * blocks * WINDOW,
            bytes_accessed=400_000_000 if kept else 100_000_000,
            transcendentals=HEADS * tokens * tokens * blocks,
        ),
        name="attention_backward",
    )(place, query, d_out, lse_rows, *kv_blocks, *kept, *given, *rows)
    first = 1 + len(own)
    return results[0], list(results[1:first]), list(results[first:first + len(kept)]), results[-1]


def last_kernel(reduction, going, early, layers, *refs):
    arrays, items = len(reduction.arrays), len(going.items)
    kept, given, refs = refs[:arrays], refs[arrays:2 * arrays], refs[2 * arrays:]
    rows, refs = refs[:items], refs[items:]
    sums, refs = (refs[:early], refs[early:2 * early]), refs[2 * early:]
    results, refs = refs[:arrays], refs[arrays:]
    homes, refs = refs[:going.count], refs[going.count:]
    other_half, refs = refs[:early + 1], refs[early + 1:]
    half_send, half_recv, chunk_send, chunk_recv = refs[:4]
    going.bind(rows, homes, refs[4:7])
    reduction.bind(kept, given, results, refs[7:])
    core = lax.axis_index("section")
    first_core = core == 0
    reduction.open()
    greet(*reduction.peers(), *going.peers())
    reduction.give(0)
    reduction.give(1)

    def half(i, layer):
        return remote_copy(sums[layer][i], other_half[i], half_send.at[i], half_recv.at[i], section=1 - core)

    def late_half(c):
        array, row, size = reduction.chunks[c]
        return remote_copy(
            results[array].at[pl.ds(row, size)],
            other_half[early].at[pl.ds(row, size)],
            chunk_send.at[c],
            chunk_recv.at[c],
            section=1 - core,
        )

    def settled(c):
        layer = layers[reduction.chunks[c][0]]
        if layer is not None:
            pl.when(core != layer)(late_half(c).start)

    reduction.settled = settled

    @pl.when(first_core)
    def second_layer():
        for i in range(early):
            half(i, 1).start()

    @pl.when(jnp.logical_not(first_core))
    def first_layer():
        for i in range(early):
            half(i, 0).start()

    going.start()
    for turn in reduction.turns():
        turn()
    for i in range(early):
        half(i, 0).wait()
    for c, (array, _, _) in enumerate(reduction.chunks):
        layer = layers[array]
        if layer is not None:
            pl.when(core != layer)(late_half(c).wait_send)
            pl.when(core == layer)(late_half(c).wait_recv)

    going.finish()


def reduce_last(kept, given, parts, layers, rows, first_sums, second_sums):
    reduction = Reduction(kept, parts)
    going = Homes([(0, 0)])
    early = len(first_sums)
    late = kept[layers.index(0)]
    halves = [jax.ShapeDtypeStruct(v.shape, v.dtype) for v in first_sums]
    halves.append(jax.ShapeDtypeStruct(late.shape[1:], late.dtype))
    n = reduction.count
    dma = pltpu.SemaphoreType.DMA
    out = pl.pallas_call(
        functools.partial(last_kernel, reduction, going, early, layers),
        out_shape=reduction.out_shapes() + going.out_shapes(rows) + tuple(halves),
        in_specs=any_specs(2 * len(kept) + 1 + 2 * early),
        out_specs=tuple(vmem_specs(len(kept)) + any_specs(early + 2)),
        scratch_shapes=[dma((early,)), dma((early,)), dma((n,)), dma((n,))] + going.scratch() + reduction.scratch(),
        compiler_params=pltpu.CompilerParams(
            collective_id=2, has_side_effects=True, vmem_limit_bytes=VMEM_LIMIT
        ),
        cost_estimate=pl.CostEstimate(flops=0, bytes_accessed=400_000_000, transcendentals=0),
        name="reduce_last",
    )(*kept, *given, rows, *first_sums, *second_sums)
    out = list(out)
    return out[:len(kept)], out[len(kept)], out[len(kept) + 1:]


def finish_kernel(parts, *refs):
    kinds = len(parts)
    first, second, other, targets, refs = refs[:kinds], refs[kinds:2 * kinds], refs[2 * kinds:3 * kinds], refs[3 * kinds:4 * kinds], refs[4 * kinds:]
    own, rest, stages, refs = refs[:kinds], refs[kinds:2 * kinds], refs[2 * kinds:3 * kinds], refs[3 * kinds:]
    sems, own_sems, rest_sems = refs
    first_core = lax.axis_index("section") == 0
    for k in range(kinds):
        pl.when(first_core)(pltpu.make_async_copy(first[k], own[k], own_sems.at[k]).start)
        pl.when(jnp.logical_not(first_core))(pltpu.make_async_copy(second[k], own[k], own_sems.at[k]).start)
        pltpu.make_async_copy(other[k], rest[k], rest_sems.at[k]).start()
    for k in range(kinds):
        rows, columns = targets[k].shape
        blocks = max(parts[k], 1)
        half, padded = first[k].shape[0], first[k].shape[1] // blocks
        size = columns // blocks
        pltpu.make_async_copy(first[k], own[k], own_sems.at[k]).wait()
        pltpu.make_async_copy(other[k], rest[k], rest_sems.at[k]).wait()

        def put(top, bottom, k=k, rows=rows, blocks=blocks, half=half, padded=padded, size=size):
            for b in range(blocks):
                here = pl.ds(b * size, size)
                stages[k][pl.ds(0, half), here] = top[:, pl.ds(b * padded, padded)].astype(f32)[:, :size]
                stages[k][pl.ds(half, rows - half), here] = bottom[:, pl.ds(b * padded, padded)].astype(f32)[:rows - half, :size]

        pl.when(first_core)(functools.partial(put, own[k], rest[k]))
        pl.when(jnp.logical_not(first_core))(functools.partial(put, rest[k], own[k]))
        pltpu.make_async_copy(stages[k], targets[k], sems.at[k]).start()
    for k in range(kinds):
        pltpu.make_async_copy(stages[k], targets[k], sems.at[k]).wait()


def finish(first, second, other, shapes, parts):
    kinds = len(first)
    return pl.pallas_call(
        functools.partial(finish_kernel, parts),
        out_shape=tuple(jax.ShapeDtypeStruct(s, f32) for s in shapes),
        in_specs=any_specs(3 * kinds),
        out_specs=tuple(any_specs(kinds)),
        scratch_shapes=[pltpu.VMEM(v.shape, bf16) for v in first] * 2
        + [pltpu.VMEM(s, f32) for s in shapes]
        + [pltpu.SemaphoreType.DMA((kinds,))] * 3,
        compiler_params=pltpu.CompilerParams(vmem_limit_bytes=VMEM_LIMIT),
        name="finish",
    )(*first, *second, *other)


def padded_shape(weight, parts):
    rows, columns = weight.shape
    rows = round_up(rows, LANES) if parts == 0 else round_up(rows, 32)
    return rows, columns if parts < 2 else parts * round_up(columns // parts, LANES)


STAGE_ROWS = 9


class Gather:
    def __init__(self, masters, parts, over_seq):
        self.parts, self.kinds, self.over_seq = parts, len(masters), over_seq
        self.shapes = [padded_shape(m, p) for m, p in zip(masters, parts)]
        self.wide_shapes = []
        for m in masters:
            rows = round_up(-(-m.shape[0] // STAGE_ROWS), 16)
            self.wide_shapes.append((2, rows, m.shape[1]))

    def out_shapes(self, ranks):
        return tuple(jax.ShapeDtypeStruct((ranks,) + s, bf16) for s in self.shapes) * 2

    def scratch(self):
        dma = pltpu.SemaphoreType.DMA
        n = 2 * self.kinds
        return (
            [pltpu.VMEM(s, f32) for s in self.wide_shapes]
            + [pltpu.VMEM(s, bf16) for s in self.shapes] * 2
            + [dma((self.kinds, 2)), dma((n,)), dma((n, 10)), dma((n, 10))]
        )

    def bind(self, masters, whole, scratch):
        n = self.kinds
        self.masters, self.whole = masters, whole
        self.wide, self.shares, self.got = scratch[:n], scratch[n:2 * n], scratch[2 * n:3 * n]
        self.wide_sem, self.own_sem, self.send, self.recv = scratch[3 * n:]
        self.core = lax.axis_index("section")
        self.rank = lax.axis_index("dp")
        z = lax.axis_index("seq")
        self.near, self.far, self.across = partners()
        self.parity = lax.rem(z, 2)
        self.pair_z = z + 1 - 2 * self.parity

    def peers(self):
        return [{"dp": self.near}, {"dp": self.far}, {"seq": self.pair_z}, {"section": 1 - self.core}]

    def rows_of(self, u, start, size):
        half = self.whole[u].shape[1] // 2
        return pl.ds(pl.multiple_of(self.core * half + start, 16), size)

    def copy(self, u, k, block, start, size, **place):
        ref = self.whole[u].at[block, self.rows_of(u, start, size)]
        return remote_copy(ref, ref, self.send.at[u, k], self.recv.at[u, k], **place)

    def sizes(self, u):
        half = self.whole[u].shape[1] // 2
        rest = round_up(half * self.over_seq[u] // 9, 16)
        return half - rest, rest

    def to_dp(self, u, k, source=None):
        size, rest = self.sizes(u)
        block, place = ((self.rank, self.near), (self.rank, self.far), (self.far, self.near))[k]
        rows = self.rows_of(u, self.parity * rest, size)
        target = self.whole[u].at[block, rows]
        source = target if source is None else source.at[rows]
        return remote_copy(source, target, self.send.at[u, k], self.recv.at[u, k], dp=place)

    def to_pair(self, u, k):
        size, rest = self.sizes(u)
        block = (self.near, self.far, self.across)[k]
        return self.copy(u, 3 + k, block, self.parity * size, rest, seq=self.pair_z)

    def to_core(self, u, k):
        half = self.whole[u].shape[1] // 2
        return self.copy(u, 6 + k, (self.near, self.far, self.across)[k], 0, half, section=1 - self.core)

    def given(self, u):
        kind = u % self.kinds
        return remote_copy(
            self.shares[kind], self.got[kind], self.send.at[u, 9], self.recv.at[u, 9], section=1 - self.core
        )

    def kept(self, u, source):
        return pltpu.make_async_copy(source[u % self.kinds], self.whole[u].at[self.rank], self.own_sem.at[u])

    def stages(self, kind):
        rows, step = self.masters[kind].shape[0], self.wide_shapes[kind][1]
        return [(i % 2, a, min(step, rows - a)) for i, a in enumerate(range(0, rows, step))]

    def load(self, kind, stage):
        slot, first, size = stage
        return pltpu.make_async_copy(
            self.masters[kind].at[pl.ds(first, size)],
            self.wide[kind].at[slot, pl.ds(0, size)],
            self.wide_sem.at[kind, slot],
        )

    def open(self):
        for kind in range(self.kinds):
            for stage in self.stages(kind)[:2]:
                self.load(kind, stage).start()

    def cast(self, kind):
        share, wide = self.shares[kind], self.wide[kind]
        blocks = max(self.parts[kind], 1)
        size, padded = wide.shape[2] // blocks, share.shape[1] // blocks
        share[...] = jnp.zeros(share.shape, bf16)
        stages = self.stages(kind)
        for i, (slot, first, count) in enumerate(stages):
            self.load(kind, stages[i]).wait()
            for b in range(blocks):
                value = wide[slot, pl.ds(0, count), b * size:(b + 1) * size]
                share[pl.ds(first, count), pl.ds(b * padded, size)] = value.astype(bf16)
            if i + 2 < len(stages):
                self.load(kind, stages[i + 2]).start()

    def first(self, u):
        if u < self.kinds:
            self.cast(u)
            pl.when(self.core == 0)(self.given(u).start)
        if 2 <= u < self.kinds + 2:
            pl.when(self.core == 1)(self.given(u + 2).start)

        def send_from(source):
            self.to_dp(u, 1, source[u % self.kinds]).start()
            self.to_dp(u, 0, source[u % self.kinds]).start()
            self.kept(u, source).start()

        @pl.when(self.core == u // self.kinds)
        def own():
            send_from(self.shares)

        @pl.when(self.core != u // self.kinds)
        def other():
            self.given(u).wait_recv()
            send_from(self.got)

    def second(self, u):
        self.to_dp(u, 1).wait_recv()
        self.to_dp(u, 2).start()
        self.to_pair(u, 1).start()
        self.to_dp(u, 0).wait_recv()
        self.to_pair(u, 0).start()

    def third(self, u):
        self.to_dp(u, 2).wait_recv()
        self.to_pair(u, 2).start()
        for k in (1, 0):
            self.to_pair(u, k).wait_recv()
            self.to_core(u, k).start()

    def fourth(self, u):
        self.to_pair(u, 2).wait_recv()
        self.to_core(u, 2).start()

    def last(self, u):
        for k in range(3):
            self.to_core(u, k).wait()
            self.to_pair(u, k).wait_send()
        self.to_dp(u, 0, self.shares[u % self.kinds]).wait_send()
        self.to_dp(u, 1, self.shares[u % self.kinds]).wait_send()
        self.to_dp(u, 2).wait_send()
        self.kept(u, self.shares).wait()

        @pl.when(self.core == u // self.kinds)
        def gave():
            self.given(u).wait_send()

    def turns(self):
        steps = (self.first, self.second, self.third, self.fourth, self.last)
        units = 2 * self.kinds

        def turn(number):
            for lag, step in enumerate(steps):
                if 0 <= number - lag < units:
                    step(number - lag)

        return [functools.partial(turn, number) for number in range(units + len(steps) - 1)]


def gather_kernel(gather, *refs):
    kinds = gather.kinds
    gather.bind(refs[:kinds], refs[kinds:3 * kinds], refs[3 * kinds:])
    gather.open()
    greet(*gather.peers())
    for turn in gather.turns():
        turn()


def gather_weights(masters, parts, ranks):
    kinds = len(masters)
    gather = Gather(masters, parts, (3,) * (2 * kinds))
    results = pl.pallas_call(
        functools.partial(gather_kernel, gather),
        out_shape=gather.out_shapes(ranks),
        in_specs=any_specs(kinds),
        out_specs=tuple(any_specs(2 * kinds)),
        scratch_shapes=gather.scratch(),
        compiler_params=pltpu.CompilerParams(
            collective_id=1, has_side_effects=True, vmem_limit_bytes=VMEM_LIMIT
        ),
        cost_estimate=pl.CostEstimate(flops=0, bytes_accessed=700_000_000, transcendentals=0),
        name="gather_weights",
    )(*masters)
    return results[:kinds], results[kinds:]


def norm_parts(values):
    center = values - jnp.mean(values, axis=-1, keepdims=True)
    inverse = lax.rsqrt(jnp.mean(center * center, axis=-1, keepdims=True) + EPS)
    return center * inverse, inverse


def norm_back(values, gain, upstream):
    unit, inverse = norm_parts(values)
    weighted = upstream * gain
    grad = inverse * (
        weighted
        - jnp.mean(weighted, axis=-1, keepdims=True)
        - unit * jnp.mean(weighted * unit, axis=-1, keepdims=True)
    )
    return grad, jnp.sum(upstream * unit, axis=0, keepdims=True), jnp.sum(upstream, axis=0, keepdims=True)


def block_loads(source, target, sems, row):
    return [
        pltpu.make_async_copy(source.at[b], target.at[b], sems.at[row, b]) for b in range(source.shape[0])
    ]


def split_columns(target, value):
    ranks, _, padded = target.shape
    share = value.shape[1] // ranks
    target[...] = jnp.zeros(target.shape, target.dtype)
    for b in range(ranks):
        target[b, :, pl.ds(0, share)] = value[:, b * share:(b + 1) * share]


def join_columns(target, parts):
    share = target.shape[1] // len(parts)
    for b, part in enumerate(parts):
        target[:, b * share:(b + 1) * share] = part[:, :share]


def qkv_kernel(h_ref, norm_ref, w_ref, a_ref, q_ref, kv_ref, w_mem, sems):
    ranks = w_ref.shape[0]
    loads = block_loads(w_ref, w_mem, sems, 0)
    load_all(loads)
    unit, _ = norm_parts(h_ref[...].astype(f32))
    split_columns(a_ref, (unit * norm_ref[0:1] + norm_ref[2:3]).astype(bf16))
    block = q_ref.shape[1]
    for copy in loads:
        copy.wait()
    for part, target in enumerate((q_ref, kv_ref.at[0], kv_ref.at[1])):
        total = sum_of([dot_nn(a_ref[b], w_mem[b, :, pl.ds(part * block, block)]) for b in range(ranks)])
        target[...] = total.astype(bf16)


def project_qkv(hidden, norm, weight):
    tokens = hidden.shape[0]
    ranks, rows, columns = weight.shape
    return pl.pallas_call(
        qkv_kernel,
        out_shape=(
            jax.ShapeDtypeStruct((ranks, tokens, rows), bf16),
            jax.ShapeDtypeStruct((tokens, columns // 3), bf16),
            jax.ShapeDtypeStruct((2, tokens, columns // 3), bf16),
        ),
        in_specs=vmem_specs(2) + any_specs(1),
        out_specs=tuple(vmem_specs(3)),
        scratch_shapes=[pltpu.VMEM(weight.shape, bf16), pltpu.SemaphoreType.DMA((1, ranks))],
        compiler_params=pltpu.CompilerParams(vmem_limit_bytes=VMEM_LIMIT),
        cost_estimate=pl.CostEstimate(
            flops=2 * tokens * weight.size, bytes_accessed=2 * weight.size, transcendentals=tokens
        ),
        name="project_qkv",
    )(hidden, norm, weight)


def mlp_kernel(
    o_ref, h_ref, norm_ref, wo_ref, wf_ref, wp_ref,
    ob_ref, r_ref, c_ref, slope_ref, g_ref, out_ref,
    wo, wf, wp, sems,
):
    ranks = wo.shape[0]
    loads = [block_loads(s, t, sems, i) for i, (s, t) in enumerate(((wo_ref, wo), (wf_ref, wf), (wp_ref, wp)))]
    for some in loads:
        load_all(some)
    split_columns(ob_ref, o_ref[:, pl.ds(0, h_ref.shape[1])])
    for copy in loads[0]:
        copy.wait()
    r_ref[...] = h_ref[...].astype(f32) + sum_of([dot_nn(ob_ref[b], wo[b]) for b in range(ranks)])
    unit, _ = norm_parts(r_ref[...])
    split_columns(c_ref, (unit * norm_ref[1:2] + norm_ref[3:4]).astype(bf16))
    for copy in loads[1]:
        copy.wait()
    block = g_ref.shape[2]
    step = block // 3

    def columns(i, carry):
        at = pl.multiple_of(i * step, LANES)
        pre = sum_of([dot_nn(c_ref[b], wf[b, :, pl.ds(at, step)]) for b in range(ranks)])
        within = pl.ds(pl.multiple_of(lax.rem(i, 3) * step, LANES), step)
        g_ref[i // 3, :, within], slope_ref[i // 3, :, within] = gelu_parts(pre)
        return carry

    lax.fori_loop(0, 3 * ranks, columns, 0)
    for copy in loads[2]:
        copy.wait()
    out_ref[...] = (r_ref[...] + sum_of([dot_nn(g_ref[b], wp[b]) for b in range(ranks)])).astype(bf16)


def out_and_mlp(attended, hidden, norm, w_out, w_fc, w_proj):
    tokens, width = hidden.shape
    ranks, rows, _ = w_out.shape
    ff = w_proj.shape[1]
    flat = jax.ShapeDtypeStruct((ranks, tokens, rows), bf16)
    size = w_out.size + w_fc.size + w_proj.size
    return pl.pallas_call(
        mlp_kernel,
        out_shape=(
            flat,
            jax.ShapeDtypeStruct((tokens, width), f32),
            flat,
            jax.ShapeDtypeStruct((ranks, tokens, ff), f32),
            jax.ShapeDtypeStruct((ranks, tokens, ff), bf16),
            jax.ShapeDtypeStruct((tokens, width), bf16),
        ),
        in_specs=vmem_specs(3) + any_specs(3),
        out_specs=tuple(vmem_specs(6)),
        scratch_shapes=[
            pltpu.VMEM(w_out.shape, bf16),
            pltpu.VMEM(w_fc.shape, bf16),
            pltpu.VMEM(w_proj.shape, bf16),
            pltpu.SemaphoreType.DMA((3, ranks)),
        ],
        compiler_params=pltpu.CompilerParams(vmem_limit_bytes=VMEM_LIMIT),
        cost_estimate=pl.CostEstimate(
            flops=2 * tokens * size, bytes_accessed=2 * size, transcendentals=2 * tokens * ff * ranks
        ),
        name="out_and_mlp",
    )(attended, hidden, norm, w_out, w_fc, w_proj)


def gelu_parts(pre):
    below = 0.5 * (1.0 + lax.erf(pre * math.sqrt(0.5)))
    slope = below + pre * (jnp.exp(-0.5 * pre * pre) * (1.0 / math.sqrt(2.0 * math.pi)))
    return (pre * below).astype(bf16), slope


FORWARD_ORDER = (
    "f0", "f1", "s0", "f2", "t0", "s1", "40", "s2", "f3", "l0", "Q0", "f4", "S0", "t1", "A00", "f5", "s3",
    "s4", "f6", "A01", "t2", "A02", "41", "s5", "f7", "A03", "t3", "43", "l1", "O", "s6", "42", "l2", "l3",
    "W", "M", "B0", "t4", "B1", "B2", "44", "t5", "s7", "B3", "l4", "t6", "45", "Q1", "t7", "S1", "46", "47",
    "l6", "l5", "A10", "l7", "A11", "A12", "A13",
)
FORWARD_OVER_SEQ = (3, 2, 3, 2, 3, 2, 2, 2)


def forward_kernel(gather, place, in_ref, cot_in, norm_ref, *refs):
    kinds = gather.kinds
    masters, refs = refs[:kinds], refs[kinds:]
    whole, refs = refs[:2 * kinds], refs[2 * kinds:]
    (a_ref, q_ref, kv_ref, *others), refs = refs[:6], refs[6:]
    (lse_ref, ob_ref, r_ref, c_ref, slope_ref, g_ref, out_ref), refs = refs[:7], refs[7:]
    (h_ref, cot_ref, next_a, next_q, next_kv, *next_others), refs = refs[:8], refs[8:]
    (next_lse, next_o), refs = refs[:2], refs[2:]
    (rows_send, rows_recv, bias, links_send, links_recv, next_send, next_recv, total, columns_mem, rows_mem, wo, slopes, gs), refs = refs[:13], refs[13:]
    (columns_sem, rows_sem, wo_sem, out_sem), refs = refs[:4], refs[4:]
    gather.bind(masters, whole, refs)
    gather.open()
    core = lax.axis_index("section")
    z = lax.axis_index("seq")
    group = z // 2
    swapped = z + 2 - 4 * group
    greet(*gather.peers(), {"seq": swapped})
    moves = ((in_ref, h_ref), (cot_in, cot_ref))

    def stay(i):
        return pltpu.make_async_copy(moves[i][0].at[group], moves[i][1], rows_send.at[i])

    def move(i):
        return remote_copy(moves[i][0].at[1 - group], moves[i][1], rows_send.at[i], rows_recv.at[i], seq=swapped)

    def rows_arrive(i):
        pl.when(core == 0)(stay(i).wait)
        pl.when(core == 1)(move(i).wait)

    for i in range(2):
        pl.when(core == 0)(stay(i).start)
        pl.when(core == 1)(move(i).start)
    ranks, tokens, rows = a_ref.shape
    block = q_ref.shape[1]

    def load_columns(weight, part):
        slot = part % 2
        return [
            pltpu.make_async_copy(
                weight.at[b, :, pl.ds(part * block, block)], columns_mem.at[slot, b], columns_sem.at[slot, b]
            )
            for b in range(ranks)
        ]

    def load_rows(weight, b):
        return [pltpu.make_async_copy(weight.at[b], rows_mem.at[b % 2], rows_sem.at[b % 2])]

    def wait_all(copies):
        for copy in copies:
            copy.wait()

    def project(hidden, norms, weight, a, q, kv):
        for part in range(2):
            load_all(load_columns(weight, part))
        unit, _ = norm_parts(hidden)
        split_columns(a, (unit * norms[0:1] + norms[2:3]).astype(bf16))
        for part, target in enumerate((q, kv.at[0], kv.at[1])):
            wait_all(load_columns(weight, part))
            target[...] = sum_of([dot_nn(a[b], columns_mem[part % 2, b]) for b in range(ranks)]).astype(bf16)
            if part == 0:
                load_all(load_columns(weight, 2))

    def put_out(b):
        slot = b % 2
        return [
            pltpu.make_async_copy(slopes.at[slot], slope_ref.at[b], out_sem.at[slot, 0]),
            pltpu.make_async_copy(gs.at[slot], g_ref.at[b], out_sem.at[slot, 1]),
        ]

    def mlp_block(b):
        slot = b % 2
        if b >= 2:
            wait_all(put_out(b - 2))
        wait_all(load_columns(whole[2], b))
        third = block // 3

        def some_columns(i, carry):
            at = pl.ds(pl.multiple_of(i * third, LANES), third)
            pre = sum_of([dot_nn(c_ref[k], columns_mem[slot, k, :, at]) for k in range(ranks)])
            gs[slot, :, at], slopes[slot, :, at] = gelu_parts(pre)
            return carry

        lax.fori_loop(0, 3, some_columns, 0)
        load_all(put_out(b))
        if b + 2 < ranks:
            load_all(load_columns(whole[2], b + 2))
        wait_all(load_rows(whole[3], b))
        total[...] = total[...] + dot_nn(gs[slot], rows_mem[slot])
        if b + 2 < ranks:
            load_all(load_rows(whole[3], b + 2))

    def attention(layer):
        if layer == 0:
            return attention_steps(
                place, q_ref, [kv_ref] + others, next_o, lse_ref, bias, (links_send, links_recv)
            )
        return attention_steps(
            place, next_q, [next_kv] + next_others, next_o, next_lse, bias, (next_send, next_recv)
        )

    out_loads = [pltpu.make_async_copy(whole[1].at[b], wo.at[b], wo_sem.at[b]) for b in range(ranks)]

    def middle():
        split_columns(ob_ref, next_o[:, pl.ds(0, h_ref.shape[1])])
        wait_all(out_loads)
        r_ref[...] = h_ref[...].astype(f32) + sum_of([dot_nn(ob_ref[b], wo[b]) for b in range(ranks)])
        unit, _ = norm_parts(r_ref[...])
        split_columns(c_ref, (unit * norm_ref[0, 1:2] + norm_ref[0, 3:4]).astype(bf16))
        total[...] = r_ref[...]

    def qkv(layer):
        if layer == 0:
            rows_arrive(0)
            project(h_ref[...].astype(f32), norm_ref.at[0], whole[0], a_ref, q_ref, kv_ref)
            return
        for b in range(2, ranks):
            wait_all(put_out(b))
        out_ref[...] = total[...].astype(bf16)
        project(out_ref[...].astype(f32), norm_ref.at[1], whole[kinds], next_a, next_q, next_kv)

    steps = {"f": gather.first, "s": gather.second, "t": gather.third, "4": gather.fourth, "l": gather.last}
    steps.update({"Q": qkv, "S": lambda layer: attention(layer)[0](), "B": mlp_block})
    for step in FORWARD_ORDER:
        if step == "M":
            middle()
        elif step == "O":
            load_all(out_loads)
        elif step == "W":
            for b in range(2):
                load_all(load_columns(whole[2], b))
                load_all(load_rows(whole[3], b))
        elif step[0] == "A":
            attention(int(step[1]))[1](int(step[2]))
        else:
            steps[step[0]](int(step[1]))
    for layer in range(2):
        attention(layer)[2]()
    rows_arrive(1)


def gather_and_forward(place, rows_in, rows_cot, norms, masters, parts, ranks):
    _, tokens, width = rows_in.shape
    kinds = len(masters)
    gather = Gather(masters, parts, FORWARD_OVER_SEQ)
    shapes = gather.shapes
    rows, block = shapes[1][0], shapes[0][1] // 3
    ff = shapes[3][0]

    def array(dtype, *shape):
        return jax.ShapeDtypeStruct(shape, dtype)

    flat, two = array(bf16, ranks, tokens, rows), array(bf16, 2, tokens, block)
    one = array(bf16, tokens, block)
    saved = (flat, one, two, two, two, two, array(f32, tokens, LANES), flat, array(f32, tokens, width), flat)
    wide = (array(f32, ranks, tokens, ff), array(bf16, ranks, tokens, ff))
    hidden = array(bf16, tokens, width)
    after = (hidden, hidden, hidden, flat, one, two, two, two, two, array(f32, tokens, LANES), one)
    dma = pltpu.SemaphoreType.DMA
    links = dma((len(HEAD_GROUPS), 3))
    out = pl.pallas_call(
        functools.partial(forward_kernel, gather),
        out_shape=gather.out_shapes(ranks) + saved + wide + after,
        in_specs=[pl.BlockSpec(memory_space=pltpu.SMEM)] + any_specs(2) + vmem_specs(1) + any_specs(kinds),
        out_specs=tuple(
            any_specs(2 * kinds)
            + vmem_specs(len(saved))
            + any_specs(2)
            + vmem_specs(2)
            + any_specs(1)
            + vmem_specs(len(after) - 3)
        ),
        scratch_shapes=[
            dma((2,)),
            dma((2,)),
            pltpu.VMEM((LINKED, tokens, tokens), f32),
            links,
            links,
            links,
            links,
            pltpu.VMEM((tokens, width), f32),
            pltpu.VMEM((2, ranks, rows, block), bf16),
            pltpu.VMEM((2, ff, width), bf16),
            pltpu.VMEM((ranks, rows, width), bf16),
            pltpu.VMEM((2, tokens, ff), f32),
            pltpu.VMEM((2, tokens, ff), bf16),
            dma((2, ranks)),
            dma((2,)),
            dma((ranks,)),
            dma((2, 2)),
        ]
        + gather.scratch(),
        compiler_params=pltpu.CompilerParams(
            collective_id=1, has_side_effects=True, vmem_limit_bytes=VMEM_LIMIT
        ),
        cost_estimate=pl.CostEstimate(flops=0, bytes_accessed=700_000_000, transcendentals=0),
        name="gather_and_forward",
    )(place, rows_in, rows_cot, norms, *masters)
    weights, out = (out[:kinds], out[kinds:2 * kinds]), out[2 * kinds:]
    normed, query, own, along, beside, both, lse, attended, residual, second, slope, activated, *out = out
    result, hidden, cotangent, *out = out
    saved = (hidden, normed, query, [own, along, beside, both], attended, lse, residual, second, slope, activated)
    normed, query, own, along, beside, both, lse, attended = out
    return weights, cotangent, saved, result, (normed, query, [own, along, beside, both], lse, attended)


class Writer:
    def __init__(self, slots, sems):
        self.slots, self.sems, self.last = slots, sems, [(), ()]
        self.turn = 0

    def put(self, make, keep, give):
        slot = self.turn % 2
        self.turn += 1
        for copy in self.last[slot]:
            copy.wait()
        make(self.slots.at[slot])
        core = lax.axis_index("section")
        half = self.slots.shape[1] // 2
        copies = []
        for i, (target, which) in enumerate(((keep, core), (give, 1 - core))):
            part = self.slots.at[slot, pl.ds(pl.multiple_of(which * half, 16), half)]
            copies.append(pltpu.make_async_copy(part, target, self.sems.at[slot, i]))
        load_all(copies)
        self.last[slot] = copies

    def finish(self):
        for copies in self.last:
            for copy in copies:
                copy.wait()


def all_rows(value, weight):
    ranks, rows, columns = weight.shape
    product = dot_nt(value, weight[...].reshape(ranks * rows, columns))
    return [product[:, b * rows:(b + 1) * rows] for b in range(ranks)]


def product_into(stage, left, right, step):
    columns = right.shape[1]
    for a in range(0, columns, step):
        n = min(step, columns - a)
        stage[:, pl.ds(a, n)] = dot_tn(left[...], right[:, pl.ds(a, n)]).astype(bf16)


def mlp_back_kernel(
    e_ref, slope_ref, g_ref, c_ref, ob_ref, r_ref, norm_ref, wo_ref, wf_ref, wp_ref,
    res_ref, att_ref, vec_ref, p_keep, p_give, f_keep, f_give, o_keep, o_give,
    wo, wf, wp, slopes, gs, block_sems, pre, d_sec, branch, att_mem, p_slots, f_slots, o_slots, sems, p_sems, f_sems, o_sems,
):
    ranks = wo.shape[0]
    loads = [block_loads(s, t, sems, i) for i, (s, t) in enumerate(((wp_ref, wp), (wf_ref, wf), (wo_ref, wo)))]
    others = [block_loads(s, t, block_sems, i) for i, (s, t) in enumerate(((slope_ref, slopes), (g_ref, gs)))]
    for b in range(ranks):
        load_all([loads[0][b], others[0][b], others[1][b]])
    for some in loads[1:]:
        load_all(some)
    writer = Writer(p_slots, p_sems)
    rows, ff = c_ref.shape[2], g_ref.shape[2]
    width = e_ref.shape[1]
    for b in range(ranks):
        loads[0][b].wait()
        others[0][b].wait()
        others[1][b].wait()
        pre[:, pl.ds(b * ff, ff)] = (dot_nt(e_ref[...], wp[b]) * slopes[b]).astype(bf16)
        writer.put(
            lambda s, b=b: product_into(s, gs.at[b], e_ref, width), p_keep.at[b], p_give.at[b]
        )
    for b in range(ranks):
        loads[1][b].wait()
    join_columns(d_sec, all_rows(pre[...], wf))
    grad, gain, bias = norm_back(r_ref[...], norm_ref[1:2], d_sec[...])
    vec_ref[0:1] = gain
    vec_ref[1:2] = bias
    total = e_ref[...].astype(f32) + grad
    res_ref[...] = total
    branch[...] = total.astype(bf16)
    for b in range(ranks):
        loads[2][b].wait()
    join_columns(att_mem, all_rows(branch[...], wo))
    att_ref[...] = jnp.zeros(att_ref.shape, bf16)
    att_ref[:, pl.ds(0, width)] = att_mem[...].astype(bf16)
    f_writer = Writer(f_slots, f_sems)
    o_writer = Writer(o_slots, o_sems)
    for b in range(ranks):
        f_writer.put(
            lambda s, b=b: product_into(s, c_ref.at[b], pre, ff), f_keep.at[b], f_give.at[b]
        )
        o_writer.put(
            lambda s, b=b: product_into(s, ob_ref.at[b], branch, width), o_keep.at[b], o_give.at[b]
        )
    writer.finish()
    f_writer.finish()
    o_writer.finish()


def half_rows(weight):
    return jax.ShapeDtypeStruct((weight.shape[0], weight.shape[1] // 2, weight.shape[2]), bf16)


def mlp_back(upstream, slope, activated, second, attended, residual, norm, w_out, w_fc, w_proj):
    tokens, width = upstream.shape
    ranks, rows, _ = w_out.shape
    size = w_out.size + w_fc.size + w_proj.size
    return pl.pallas_call(
        mlp_back_kernel,
        out_shape=(
            jax.ShapeDtypeStruct((tokens, width), f32),
            jax.ShapeDtypeStruct((tokens, round_up(width, LANES)), bf16),
            jax.ShapeDtypeStruct((2, width), f32),
        )
        + tuple(half_rows(w) for w in (w_proj, w_proj, w_fc, w_fc, w_out, w_out)),
        in_specs=vmem_specs(1) + any_specs(2) + vmem_specs(4) + any_specs(3),
        out_specs=tuple(vmem_specs(3) + any_specs(6)),
        scratch_shapes=[
            pltpu.VMEM(w_out.shape, bf16),
            pltpu.VMEM(w_fc.shape, bf16),
            pltpu.VMEM(w_proj.shape, bf16),
            pltpu.VMEM(slope.shape, f32),
            pltpu.VMEM(activated.shape, bf16),
            pltpu.SemaphoreType.DMA((2, ranks)),
            pltpu.VMEM((tokens, w_fc.shape[2]), bf16),
            pltpu.VMEM((tokens, width), f32),
            pltpu.VMEM((tokens, width), bf16),
            pltpu.VMEM((tokens, width), f32),
            pltpu.VMEM((2,) + w_proj.shape[1:], bf16),
            pltpu.VMEM((2,) + w_fc.shape[1:], bf16),
            pltpu.VMEM((2,) + w_out.shape[1:], bf16),
            pltpu.SemaphoreType.DMA((3, ranks)),
            pltpu.SemaphoreType.DMA((2, 2)),
            pltpu.SemaphoreType.DMA((2, 2)),
            pltpu.SemaphoreType.DMA((2, 2)),
        ],
        compiler_params=pltpu.CompilerParams(vmem_limit_bytes=VMEM_LIMIT),
        cost_estimate=pl.CostEstimate(
            flops=4 * tokens * size, bytes_accessed=4 * size, transcendentals=tokens
        ),
        name="mlp_backward",
    )(upstream, slope, activated, second, attended, residual, norm, w_out, w_fc, w_proj)


def qkv_back_kernel(
    dq_ref, dkv_ref, a_ref, h_ref, res_ref, norm_ref, w_ref,
    sent_ref, vec_ref, keep, give,
    w_mem, d_proj, d_normed, slots, sems, out_sems,
):
    ranks, rows, columns = w_ref.shape
    loads = block_loads(w_ref, w_mem, sems, 0)
    load_all(loads)
    writer = Writer(slots, out_sems)
    block = columns // 3
    d_proj[:, pl.ds(0, block)] = dq_ref[...]
    d_proj[:, pl.ds(block, block)] = dkv_ref[0]
    d_proj[:, pl.ds(2 * block, block)] = dkv_ref[1]
    for b in range(ranks):
        writer.put(
            lambda s, b=b: product_into(s, a_ref.at[b], d_proj, block), keep.at[b], give.at[b]
        )
    for copy in loads:
        copy.wait()
    join_columns(d_normed, all_rows(d_proj[...], w_mem))
    grad, gain, bias = norm_back(h_ref[...].astype(f32), norm_ref[0:1], d_normed[...])
    vec_ref[0:1] = gain
    vec_ref[1:2] = bias
    sent_ref[...] = (res_ref[...] + grad).astype(bf16)
    writer.finish()


def qkv_back(d_query, d_pair, normed, hidden, residual_grad, norm, weight):
    tokens, width = hidden.shape
    ranks, rows, columns = weight.shape
    return pl.pallas_call(
        qkv_back_kernel,
        out_shape=(
            jax.ShapeDtypeStruct((tokens, width), bf16),
            jax.ShapeDtypeStruct((2, width), f32),
            half_rows(weight),
            half_rows(weight),
        ),
        in_specs=vmem_specs(6) + any_specs(1),
        out_specs=tuple(vmem_specs(2) + any_specs(2)),
        scratch_shapes=[
            pltpu.VMEM(weight.shape, bf16),
            pltpu.VMEM((tokens, columns), bf16),
            pltpu.VMEM((tokens, width), f32),
            pltpu.VMEM((2, rows, columns), bf16),
            pltpu.SemaphoreType.DMA((1, ranks)),
            pltpu.SemaphoreType.DMA((2, 2)),
        ],
        compiler_params=pltpu.CompilerParams(vmem_limit_bytes=VMEM_LIMIT),
        cost_estimate=pl.CostEstimate(
            flops=4 * tokens * weight.size, bytes_accessed=4 * weight.size, transcendentals=tokens
        ),
        name="qkv_backward",
    )(d_query, d_pair, normed, hidden, residual_grad, norm, weight)


def swap_cores(value):
    return lax.ppermute(value, "section", [(0, 1), (1, 0)])


def send_joint(value, axis, route):
    size = lax.axis_size(axis)
    pairs = []
    for core in range(2):
        for index in range(size):
            to = route(core, index)
            if to is not None:
                pairs.append((core * size + index, to[0] * size + to[1]))
    return lax.ppermute(value, ("section", axis), pairs)


def on_device(
    layer_in, cotangent, lengths, block_order, w_qkv, w_out, w_fc, w_proj, norm_gains, norm_biases
):
    tokens, width = layer_in.shape[2:]
    blocks = lax.axis_size("seq")
    ranks = lax.axis_size("dp")
    half = blocks // 2
    core = lax.axis_index("section")
    place_dp = lax.axis_index("dp")
    place_seq = lax.axis_index("seq")
    first_core = core == 0
    group = place_seq // half
    linked = blocks == LINKED and ranks == LINKED

    def per_core(left, right):
        return jnp.where(first_core, left, right)

    def after(value, *others):
        return lax.optimization_barrier((value, others))[0]

    def own_rows(value):
        value = value[:, 0]
        mine = lax.dynamic_index_in_dim(value, group, 0, False)
        other = lax.dynamic_index_in_dim(value, 1 - group, 0, False)
        moved = send_joint(other, "seq", lambda c, z: (1, z ^ half) if c == 1 else None)
        return per_core(mine, moved)

    def back_home(first, second):
        crossed = send_joint(
            per_core(second, first), "seq", lambda c, z: (1, z) if c == 0 else (0, z ^ half)
        )
        along = send_joint(second, "seq", lambda c, z: (1, z ^ half) if c == 1 else None)
        mine = per_core(first, crossed)
        other = per_core(crossed, along)
        return jnp.where(group == 0, jnp.stack([mine, other]), jnp.stack([other, mine]))

    steps = []
    bit = 1
    while bit < half:
        steps.append(bit)
        bit *= 2
    my_block = per_core(place_seq, place_seq ^ half)
    block_ids = [my_block]
    for bit in steps:
        block_ids = block_ids + [b ^ bit for b in block_ids]
    block_ids = block_ids + [b ^ half for b in block_ids]
    limit = lax.dynamic_index_in_dim(lengths[:, 0], group, 0, False)
    starts = block_order[jnp.stack(block_ids)] * tokens
    place = jnp.concatenate([limit[None], starts]).astype(jnp.int32)

    def gather_keys(own):
        parts = [own]
        for bit in steps:
            route = [(z, z ^ bit) for z in range(blocks)]
            parts = parts + [lax.ppermute(p, "seq", route) for p in parts]
        return parts + [swap_cores(p) for p in parts]

    def scatter_keys(parts):
        cut = len(parts) // 2
        moved = [swap_cores(p) for p in parts[cut:]]
        parts = [(p.astype(f32) + m.astype(f32)).astype(bf16) for p, m in zip(parts[:cut], moved)]
        for bit in reversed(steps):
            cut = len(parts) // 2
            route = [(z, z ^ bit) for z in range(blocks)]
            moved = [lax.ppermute(p, "seq", route) for p in parts[cut:]]
            parts = [(p.astype(f32) + m.astype(f32)).astype(bf16) for p, m in zip(parts[:cut], moved)]
        return parts[0]

    masters = (w_qkv[0], w_out[0], w_fc[0], w_proj[0])
    parts = (3, 1, ranks, 0)
    own_norms = jnp.concatenate([norm_gains[0], norm_biases[0]])
    other_norms = swap_cores(own_norms)
    norms = [per_core(own_norms, other_norms), per_core(other_norms, own_norms)]

    def attend(projected):
        normed, query, own_keys = projected
        keys = gather_keys(own_keys)
        attended, lse, keys = attention_forward(place, query, keys, blocks)
        return normed, query, keys, lse, attended

    def forward(hidden, layer, attention):
        _, wout, wfc, wproj = weights[layer]
        normed, query, keys, lse, attended = attention
        attended, residual, second, slope, activated, result = out_and_mlp(
            attended, hidden, norms[layer], wout, wfc, wproj
        )
        return result, (hidden, normed, query, keys, attended, lse, residual, second, slope, activated)

    if linked:
        weights, rows_cot, saved_first, first_out, attention = gather_and_forward(
            place, layer_in[:, 0], cotangent[:, 0], jnp.stack(norms), masters, parts, ranks
        )
    else:
        rows_in, rows_cot = own_rows(layer_in), own_rows(cotangent)
        weights = gather_weights(masters, parts, ranks)
        first_out, saved_first = forward(rows_in, 0, attend(project_qkv(rows_in, norms[0], weights[0][0])))
        attention = attend(project_qkv(first_out, norms[1], weights[1][0]))
    second_out, saved_second = forward(first_out, 1, attention)

    def backward(upstream, saved, layer, layers, rows):
        wqkv, wout, wfc, wproj = weights[layer]
        hidden, normed, query, keys, attended, lse, residual, second, slope, activated = saved
        d_residual, d_att, vectors_two, *mlp_grads = mlp_back(
            upstream, slope, activated, second, attended, residual, norms[layer], wout, wfc, wproj
        )
        kept, given = mlp_grads[0::2], mlp_grads[1::2]
        if linked:
            d_query, d_keys, sums, home = attention_backward(
                place, query, d_att, lse.T, keys, kept, given, (6, 5, 3), layers, rows
            )
            d_pair = d_keys[0]
        else:
            d_query, d_keys, _, home = attention_backward(place, query, d_att, lse.T, keys)
            d_pair = scatter_keys(d_keys)
            sums = plain_sums(kept, given)
        sent, vectors_one, *qkv_grads = qkv_back(d_query, d_pair, normed, hidden, d_residual, norms[layer], wqkv)
        return sent, sums, home, qkv_grads, jnp.stack([vectors_one[0], vectors_two[0], vectors_one[1], vectors_two[1]])

    def plain_sums(kept, given):
        total = [(k.astype(f32) + swap_cores(g).astype(f32)).astype(k.dtype) for k, g in zip(kept, given)]
        return [lax.psum(lax.psum_scatter(t, "dp", scatter_dimension=0), "seq") for t in total]

    def by_rank(vectors):
        return vectors.reshape(4, ranks, -1).transpose(1, 0, 2)

    second_grad, second_sums, layer_results, second_qkv, second_vectors = backward(
        rows_cot, saved_second, 1, (0, 1), (first_out, second_out)
    )
    first_grad, first_sums, grad_home, first_qkv, first_vectors = backward(
        second_grad, saved_first, 0, (1,), (second_grad,)
    )
    kept = [second_qkv[0], by_rank(per_core(first_vectors, second_vectors)), first_qkv[0]]
    given = [second_qkv[1], by_rank(per_core(second_vectors, first_vectors)), first_qkv[1]]
    if linked:
        (second_last, vectors, first_last), first_home, other = reduce_last(
            kept, given, (5, 1, 5), (1, None, 0), first_grad, first_sums, second_sums
        )
        grad_results = per_core(first_home, grad_home)
    else:
        second_last, vectors, first_last = plain_sums(kept, given)
        layer_results = back_home(first_out, second_out)
        grad_results = back_home(first_grad, second_grad)
    first_sums = list(first_sums) + [first_last]
    second_sums = list(second_sums) + [second_last]
    if not linked:
        other = [swap_cores(per_core(b, a)) for a, b in zip(first_sums, second_sums)]
    shapes = [w_proj.shape[1:], w_fc.shape[1:], w_out.shape[1:], w_qkv.shape[1:]]
    g_proj, g_fc, g_out, g_qkv = finish(first_sums, second_sums, other, shapes, (1, ranks, 1, 3))
    return (
        layer_results[None, :, None],
        grad_results[None, :, None],
        g_qkv[None],
        g_out[None],
        g_fc[None],
        g_proj[None],
        vectors[:2][None],
        vectors[2:][None],
    )


def solution(mesh):
    return jax.shard_map(
        on_device,
        mesh=mesh,
        in_specs=(
            P(None, "dp", "seq", None),
            P(None, "dp", "seq", None),
            P(None, "dp"),
            P(),
            P("section", "dp", None),
            P("section", "dp", None),
            P("section", "dp", None),
            P("section", "dp", None),
            P("section", None, None),
            P("section", None, None),
        ),
        out_specs=(
            P("section", None, "dp", "seq", None),
            P("section", None, "dp", "seq", None),
            P("section", "dp", None),
            P("section", "dp", None),
            P("section", "dp", None),
            P("section", "dp", None),
            P("section", None, "dp"),
            P("section", None, "dp"),
        ),
        check_vma=False,
    )
```

time: 2500 us -> 786 us (0.31)
  waiting for transfers between devices: 1480 us -> 0.01 us
  Pallas kernels: 0 us -> 755 us
  matrix products: 511 us -> 0 us
  other arithmetic: 250 us -> 4.79 us
  local copies, waits for them, and re-layouts: 183 us -> 15.3 us
    pallas_call x0 -> x10, Pallas kernels: none -> 755 us  [the longest x2 289 us: attention_backward(): pl.pallas_call(functools.partial(attention_backward_kernel, blocks, reduc...]
    all_gather x10 -> x0, waiting for transfers between devices: 702 us -> none  [the longest x3 200 us: forward(): lax.all_gather(projected[:, hidden_width:], 'seq', axis=0, tiled=True)]
    dot_general x93 -> x0, matrix products: 511 us -> none  [the longest x15 57.3 us: one_group(): jnp.einsum('hqd,hkd->hqk', group_q, group_k, preferred_element_type=f32)]
    unnamed x13 -> x0, waiting for transfers between devices: 388 us -> none
    psum x1 -> x0, waiting for transfers between devices: 246 us -> none  [on_device(): lax.psum(shards[3].astype(jnp.bfloat16), 'seq').astype(jnp.float32)]
    reduce_scatter x3 -> x0, waiting for transfers between devices: 143 us -> none  [attention_back(): lax.psum_scatter(jnp.concatenate([d_key, d_value], axis=1).astype(jnp.bfl...]
    sub x15 -> x0, other arithmetic: 105 us -> none  [one_group(): d_prob - row_inner[..., None]]
    dynamic_slice x36 -> x1, local copies, waits for them, and re-layouts: 62.8 us -> 1.24 us  [on_device(): limit = lax.dynamic_index_in_dim(lengths[:, 0], group, 0, False)]
  transfers between devices with their start and end apart: 24 -> 1, of which waited for: 18 -> 0; matrix products, arithmetic and copies ran while one was open for 12% -> 1% of each run, Pallas kernels for 0% -> 0%
where the time goes in v1:
time: 786 us; the launch traced here: 777 us
  Pallas kernels  755 us (96%)
  local copies, waits for them, and re-layouts  15.3 us (2%)
    pallas_call x2, Pallas kernels, attention_backward(): pl.pallas_call(functools.partial(attention_backward_kernel, blocks, reduc...  289 us
    pallas_call x1, Pallas kernels, gather_and_forward(): pl.pallas_call(functools.partial(forward_kernel, gather), out_shape=gathe...  250 us
    pallas_call x1, Pallas kernels, reduce_last(): pl.pallas_call(functools.partial(last_kernel, reduction, going, early, la...  101 us
    pallas_call x2, Pallas kernels, mlp_back(): pl.pallas_call(mlp_back_kernel, out_shape=(jax.ShapeDtypeStruct((tokens,...  60.2 us
    pallas_call x2, Pallas kernels, qkv_back(): pl.pallas_call(qkv_back_kernel, out_shape=(jax.ShapeDtypeStruct((tokens,...  25.5 us
    pallas_call x1, Pallas kernels, out_and_mlp(): pl.pallas_call(mlp_kernel, out_shape=(flat, jax.ShapeDtypeStruct((tokens,...  19.9 us
  transfers between devices with their start and end apart: 1, of which 0 were waited for; matrix products, arithmetic and copies ran while one was open for 1% of the time, Pallas kernels for 0%

profile of v1, /device:TPU:0, one launch (start us, length us, event | category | flops | bytes accessed | tf_op | source)
XLA Modules:
  0.0 776.7 jit_solution(10352560458888690887)
XLA Ops:
  0.6 0.0 copy-start
  0.6 0.7 pad_maximum_fusion.3
  1.4 0.5 collective-permute-start
  1.9 0.1 fusion
  2.0 0.0 copy-done
  2.0 0.0 copy-start.3
  2.0 0.6 gather_fusion
  2.7 1.2 constant_dynamic-slice_fusion
  3.9 1.2 pad_add_fusion.place
  5.1 2.4 copy.24
  7.5 0.0 copy-done.3
  7.5 1.4 copy.25
  8.9 0.0 collective-permute-done
  8.9 0.0 copy-done.6
  8.9 0.0 copy-done.7
  8.9 0.0 copy-start.4
  9.0 0.0 copy-start.5
  9.0 0.6 pad_maximum_fusion.norm_ref
  9.6 250.4 %gather_and_forward.1 = (bf16[4,288,3456]{2,1,0:T(8,128)(2,1)}, bf16[4,288,1120]{2,1,0:T(8,128)(2,1)}, bf16[4,288,4608]{2,1,0:T(8,128)(2,1)}, bf16[4,1152,1120]{...) custom-call(s32[5]{0:T(128)} %pad_add_fusion.place, ...), custom_call_target="tpu_custom_call" | custom-call | bytes 700000000 | tf_op jit(solution)/shard_map/gather_and_forward/pallas_call | solution.py:1272
  260.0 1.7 copy.26
  261.7 1.7 copy.27
  263.4 19.9 %out_and_mlp.1 = (bf16[4,256,288]{2,1,0:T(8,128)(2,1)}, f32[256,1120]{1,0:T(8,128)}, bf16[4,256,288]{2,1,0:T(8,128)(2,1)}, f32[4,256,1152]{2,1,0:T(8,128)}, bf16...) custom-call(bf16[256,1152]{1,0:T(8,128)(2,1)} %get-tuple-element.97.o_ref, ...), custom_call_target="tpu_custom_call" | custom-call | flops 6020923392 | bytes 23519232 | tf_op jit(solution)/shard_map/out_and_mlp/pallas_call | solution.py:1072
  283.2 30.2 %mlp_backward.2 = (f32[256,1120]{1,0:T(8,128)}, bf16[256,1152]{1,0:T(8,128)(2,1)}, f32[2,1120]{1,0:T(2,128)}, bf16[4,576,1120]{2,1,0:T(8,128)(2,1)}, bf16[4,576,...) custom-call(bf16[256,1120]{1,0:T(8,128)(2,1)} %get-tuple-element.96., ...), custom_call_target="tpu_custom_call" | custom-call | flops 12041846784 | bytes 47038464 | tf_op jit(solution)/shard_map/mlp_backward/pallas_call | solution.py:1416
  313.4 142.3 %attention_backward.2 = (bf16[256,1152]{1,0:T(8,128)(2,1)}, bf16[2,256,1152]{2,1,0:T(8,128)(2,1)}, bf16[576,1120]{1,0:T(8,128)(2,1)}, bf16[144,4608]{1,0:T(8,128...) custom-call(s32[5]{0:T(128)} %pad_add_fusion.place, bf16[256,1152]{1,0:T(8,128)(2,1)} %get-tuple-element.95.q_ref, ...), custom_call_target="tpu_custom_call" | custom-call | flops 13421772800 | bytes 400000000 | tf_op jit(solution)/shard_map/attention_backward/pallas_call | solution.py:595
  455.7 2.7 copy.28
  458.4 12.8 %qkv_backward.2 = (bf16[256,1120]{1,0:T(8,128)(2,1)}, f32[2,1120]{1,0:T(2,128)}, bf16[4,144,3456]{2,1,0:T(8,128)(2,1)}, bf16[4,144,3456]{2,1,0:T(8,128)(2,1)}) custom-call(bf16[256,1152]{1,0:T(8,128)(2,1)} %get-tuple-element.121.dq_ref, bf16[2,256,1152]{2,1,0:T(8,128)(2,1)} %get-tuple-element.122.dkv_ref, bf16[4,256,288]{2,1,0:T(8,128)(2,1)} %get-tuple-element.123.a_ref, ...), custom_call_target="tpu_custom_call" | custom-call | flops 4076863488 | bytes 15925248 | tf_op jit(solution)/shard_map/qkv_backward/pallas_call | solution.py:1483
  471.2 30.0 %mlp_backward.3 = (f32[256,1120]{1,0:T(8,128)}, bf16[256,1152]{1,0:T(8,128)(2,1)}, f32[2,1120]{1,0:T(2,128)}, bf16[4,576,1120]{2,1,0:T(8,128)(2,1)}, bf16[4,576,...) custom-call(bf16[256,1120]{1,0:T(8,128)(2,1)} %get-tuple-element.128, ...), custom_call_target="tpu_custom_call" | custom-call | flops 12041846784 | bytes 47038464 | tf_op jit(solution)/shard_map/mlp_backward/pallas_call | solution.py:1416
  501.2 147.1 %attention_backward.3 = (bf16[256,1152]{1,0:T(8,128)(2,1)}, bf16[2,256,1152]{2,1,0:T(8,128)(2,1)}, bf16[576,1120]{1,0:T(8,128)(2,1)}, bf16[144,4608]{1,0:T(8,128...) custom-call(s32[5]{0:T(128)} %pad_add_fusion.place, bf16[256,1152]{1,0:T(8,128)(2,1)} %get-tuple-element.127.q_ref, ...), custom_call_target="tpu_custom_call" | custom-call | flops 13421772800 | bytes 400000000 | tf_op jit(solution)/shard_map/attention_backward/pallas_call | solution.py:595
  648.3 0.0 copy-start.9
  648.3 0.0 copy-start.10
  648.3 0.0 copy-start.8
  648.3 12.8 %qkv_backward.3 = (bf16[256,1120]{1,0:T(8,128)(2,1)}, f32[2,1120]{1,0:T(2,128)}, bf16[4,144,3456]{2,1,0:T(8,128)(2,1)}, bf16[4,144,3456]{2,1,0:T(8,128)(2,1)}) custom-call(bf16[256,1152]{1,0:T(8,128)(2,1)} %get-tuple-element.149.dq_ref, bf16[2,256,1152]{2,1,0:T(8,128)(2,1)} %get-tuple-element.150.dkv_ref, bf16[4,256,288]{2,1,0:T(8,128)(2,1)} %get-tuple-element.151.a_ref, ...), custom_call_target="tpu_custom_call" | custom-call | flops 4076863488 | bytes 15925248 | tf_op jit(solution)/shard_map/qkv_backward/pallas_call | solution.py:1483
  661.1 0.8 slice_reduce_fusion.7
  661.9 0.1 stack.54
  662.0 0.1 stack.56
  662.1 0.1 stack.59
  662.2 0.1 stack.61
  662.3 0.1 stack.55
  662.4 0.1 stack.57
  662.5 0.1 stack.60
  662.6 0.1 stack.62
  662.7 0.7 select_bitcast_fusion.1
  663.4 101.5 %reduce_last.1 = (bf16[144,3456]{1,0:T(8,128)(2,1)}, f32[4,280]{1,0:T(4,128)}, bf16[144,3456]{1,0:T(8,128)(2,1)}, bf16[2,256,1120]{2,1,0:T(8,128)(2,1)}, bf16[57...) custom-call(bf16[4,144,3456]{2,1,0:T(8,128)(2,1)} %get-tuple-element.126., ...), custom_call_target="tpu_custom_call" | custom-call | bytes 400000000 | tf_op jit(solution)/shard_map/reduce_last/pallas_call | solution.py:693
  764.9 0.0 copy-done.2
  764.9 1.4 select_bitcast_fusion
  766.3 1.4 copy.29
  767.7 0.6 slice_bitcast_fusion
  768.3 8.2 %finish.1 = (f32[1120,1120]{1,0:T(8,128)}, f32[280,4480]{1,0:T(8,128)}, f32[280,1120]{1,0:T(8,128)}, f32[280,3360]{1,0:T(8,128)}) custom-call(bf16[576,1120]{1,0:T(8,128)(2,1)} %get-tuple-element.163.refs_7_.refs_0_, bf16[144,4608]{1,0:T(8,128)(2,1)} %get-tuple-element.164.refs_8_.refs_1_, bf16[144,1120]{1,0:T(8,128)(2,1)} %get-tuple-element.165.refs_9_.refs_2_, ...), custom_call_target="tpu_custom_call" | custom-call | tf_op jit(solution)/shard_map/finish/pallas_call | solution.py:742
  (18 shorter events, 0.1 us)
Async XLA Ops:
  0.6 1.4 copy-start
  1.4 7.5 collective-permute-start
  2.0 5.5 copy-start.3
  7.5 1.4 copy-start.6
  7.5 1.4 copy-start.7
  8.9 251.1 %copy-start.4 = (f32[4,1120]{1,0:T(4,128)}, f32[4,1120]{1,0:T(4,128)S(1)}, u32[]{:S(2)}) copy-start(f32[4,1120]{1,0:T(4,128)S(1)} %get-tuple-element.209.norm_ref) | copy-start | bytes 53764
  9.0 251.1 %copy-start.5 = (f32[4,1120]{1,0:T(4,128)}, f32[4,1120]{1,0:T(4,128)S(1)}, u32[]{:S(2)}) copy-start(f32[4,1120]{1,0:T(4,128)S(1)} %get-tuple-element.208.norm_ref) | copy-start | bytes 53764
  648.3 13.8 %copy-start.9 = (f32[2,1120]{1,0:T(2,128)S(1)}, f32[2,1120]{1,0:T(2,128)}, u32[]{:S(2)}) copy-start(f32[2,1120]{1,0:T(2,128)} %get-tuple-element.157) | copy-start | bytes 26884
  648.3 14.0 %copy-start.10 = (f32[2,1120]{1,0:T(2,128)S(1)}, f32[2,1120]{1,0:T(2,128)}, u32[]{:S(2)}) copy-start(f32[2,1120]{1,0:T(2,128)} %get-tuple-element.156) | copy-start | bytes 26884
  648.3 14.2 %copy-start.8 = (f32[2,1120]{1,0:T(2,128)S(1)}, f32[2,1120]{1,0:T(2,128)}, u32[]{:S(2)}) copy-start(f32[2,1120]{1,0:T(2,128)} %get-tuple-element.158) | copy-start | bytes 26884
  663.4 101.5 %copy-start.2 = (bf16[2,256,1120]{2,1,0:T(8,128)(2,1)S(1)}, bf16[2,256,1120]{2,1,0:T(8,128)(2,1)}, u32[]{:S(2)}) copy-start(bf16[2,256,1120]{2,1,0:T(8,128)(2,1)} %get-tuple-element.170) | copy-start | bytes 3440644
  766.3 1.4 copy-start.11
  768.3 8.2 %copy-start.1 = (s32[4]{0:T(128)S(1)}, s32[4]{0:T(128)}, u32[]{:S(2)}) copy-start(s32[4]{0:T(128)} %param.13) | copy-start | bytes 52

commit v2 on v1

--- a/solution.py
+++ b/solution.py
@@ -333,8 +333,8 @@
 HEAD_GROUPS = ((0, 6), (6, 6), (12, 6), (18, 2))
 LANES_IN = ((0, 384), (384, 384), (768, 256), (1024, 128))
 BACKWARD_ORDER = (
-    "p", "t", "p", "t", "p", "s0", "t", "p", "p", "t", "p", "s1", "a0", "t", "p", "p", "t", "p", "s2", "a1",
-    "t", "a2", "p", "s3", "t", "a3", "t", "z",
+    "p", "p", "t", "p", "s0", "p", "t", "p", "a0", "p", "t", "s1", "p", "a1", "p", "t", "p", "s2", "p", "a2",
+    "s3", "t", "t", "a3", "t", "t", "t", "z",
 )
 LANES_OUT = ((0, 256), (256, 384), (640, 256), (896, 256))
 
@@ -381,7 +381,7 @@
         bias[b] = jnp.where((column <= row) & (column < place[0]), 0.0, NEG)
 
 
-def attention_steps(place, q_ref, kv_refs, o_pad, lse_ref, bias, links):
+def attention_steps(place, q_ref, kv_refs, o_pad, lse_rows, lse_ref, bias, links):
     tokens, blocks = q_ref.shape[0], len(kv_refs)
     scale = HEAD_DIM ** -0.5
     groups = range(len(HEAD_GROUPS))
@@ -430,6 +430,7 @@
         heads_of(group, one_head)
 
     def end():
+        lse_rows[...] = jnp.transpose(lse_ref[...])
         if links:
             for group in groups:
                 for copy in copies(group):
@@ -439,11 +440,12 @@
 
 
 def attention_forward_kernel(blocks, place, q_ref, *refs):
-    o_ref, lse_ref, bias = refs[blocks:]
-    start, work, _ = attention_steps(place, q_ref, refs[:blocks], o_ref, lse_ref, bias, ())
+    o_ref, lse_rows, lse_ref, bias = refs[blocks:]
+    start, work, end = attention_steps(place, q_ref, refs[:blocks], o_ref, lse_rows, lse_ref, bias, ())
     start()
     for group in range(len(HEAD_GROUPS)):
         work(group)
+    end()
 
 
 def attention_forward(place, query, kv_blocks, blocks):
@@ -452,11 +454,11 @@
         functools.partial(attention_forward_kernel, blocks),
         out_shape=(
             jax.ShapeDtypeStruct((tokens, width), bf16),
-            jax.ShapeDtypeStruct((tokens, LANES), f32),
+            jax.ShapeDtypeStruct((LANES, tokens), f32),
         ),
         in_specs=[pl.BlockSpec(memory_space=pltpu.SMEM)] + vmem_specs(1 + len(kv_blocks)),
         out_specs=tuple(vmem_specs(2)),
-        scratch_shapes=[pltpu.VMEM((blocks, tokens, tokens), f32)],
+        scratch_shapes=[pltpu.VMEM((tokens, LANES), f32), pltpu.VMEM((blocks, tokens, tokens), f32)],
         compiler_params=pltpu.CompilerParams(vmem_limit_bytes=VMEM_LIMIT),
         cost_estimate=pl.CostEstimate(
             flops=4 * HEADS * tokens * tokens * blocks * WINDOW,
@@ -1110,15 +1112,15 @@
 FORWARD_OVER_SEQ = (3, 2, 3, 2, 3, 2, 2, 2)
 
 
-def forward_kernel(gather, place, in_ref, cot_in, norm_ref, *refs):
+def forward_kernel(gather, place, in_ref, cot_in, own_norms, *refs):
     kinds = gather.kinds
     masters, refs = refs[:kinds], refs[kinds:]
     whole, refs = refs[:2 * kinds], refs[2 * kinds:]
     (a_ref, q_ref, kv_ref, *others), refs = refs[:6], refs[6:]
     (lse_ref, ob_ref, r_ref, c_ref, slope_ref, g_ref, out_ref), refs = refs[:7], refs[7:]
-    (h_ref, cot_ref, next_a, next_q, next_kv, *next_others), refs = refs[:8], refs[8:]
+    (norm_ref, h_ref, cot_ref, next_a, next_q, next_kv, *next_others), refs = refs[:9], refs[9:]
     (next_lse, next_o), refs = refs[:2], refs[2:]
-    (rows_send, rows_recv, bias, links_send, links_recv, next_send, next_recv, total, columns_mem, rows_mem, wo, slopes, gs), refs = refs[:13], refs[13:]
+    (rows_send, rows_recv, norm_sem, lse_mem, bias, links_send, links_recv, next_send, next_recv, total, columns_mem, rows_mem, wo, slopes, gs), refs = refs[:15], refs[15:]
     (columns_sem, rows_sem, wo_sem, out_sem), refs = refs[:4], refs[4:]
     gather.bind(masters, whole, refs)
     gather.open()
@@ -1130,10 +1132,15 @@
     moves = ((in_ref, h_ref), (cot_in, cot_ref))
 
     def stay(i):
-        return pltpu.make_async_copy(moves[i][0].at[group], moves[i][1], rows_send.at[i])
+        return pltpu.make_async_copy(moves[i][0].at[group, 0], moves[i][1], rows_send.at[i])
 
     def move(i):
-        return remote_copy(moves[i][0].at[1 - group], moves[i][1], rows_send.at[i], rows_recv.at[i], seq=swapped)
+        return remote_copy(moves[i][0].at[1 - group, 0], moves[i][1], rows_send.at[i], rows_recv.at[i], seq=swapped)
+
+    norms_here = pltpu.make_async_copy(own_norms, norm_ref.at[core], norm_sem.at[0])
+    norms_there = remote_copy(own_norms, norm_ref.at[core], norm_sem.at[1], norm_sem.at[2], section=1 - core)
+    norms_here.start()
+    norms_there.start()
 
     def rows_arrive(i):
         pl.when(core == 0)(stay(i).wait)
@@ -1204,15 +1211,16 @@
     def attention(layer):
         if layer == 0:
             return attention_steps(
-                place, q_ref, [kv_ref] + others, next_o, lse_ref, bias, (links_send, links_recv)
+                place, q_ref, [kv_ref] + others, next_o, lse_ref, lse_mem, bias, (links_send, links_recv)
             )
         return attention_steps(
-            place, next_q, [next_kv] + next_others, next_o, next_lse, bias, (next_send, next_recv)
+            place, next_q, [next_kv] + next_others, next_o, next_lse, lse_mem, bias, (next_send, next_recv)
         )
 
     out_loads = [pltpu.make_async_copy(whole[1].at[b], wo.at[b], wo_sem.at[b]) for b in range(ranks)]
 
     def middle():
+        attention(0)[2]()
         split_columns(ob_ref, next_o[:, pl.ds(0, h_ref.shape[1])])
         wait_all(out_loads)
         r_ref[...] = h_ref[...].astype(f32) + sum_of([dot_nn(ob_ref[b], wo[b]) for b in range(ranks)])
@@ -1223,6 +1231,8 @@
     def qkv(layer):
         if layer == 0:
             rows_arrive(0)
+            norms_here.wait()
+            norms_there.wait()
             project(h_ref[...].astype(f32), norm_ref.at[0], whole[0], a_ref, q_ref, kv_ref)
             return
         for b in range(2, ranks):
@@ -1245,13 +1255,12 @@
             attention(int(step[1]))[1](int(step[2]))
         else:
             steps[step[0]](int(step[1]))
-    for layer in range(2):
-        attention(layer)[2]()
+    attention(1)[2]()
     rows_arrive(1)
 
 
-def gather_and_forward(place, rows_in, rows_cot, norms, masters, parts, ranks):
-    _, tokens, width = rows_in.shape
+def gather_and_forward(place, layer_in, cotangent, norms, masters, parts, ranks):
+    tokens, width = layer_in.shape[2:]
     kinds = len(masters)
     gather = Gather(masters, parts, FORWARD_OVER_SEQ)
     shapes = gather.shapes
@@ -1263,10 +1272,10 @@
 
     flat, two = array(bf16, ranks, tokens, rows), array(bf16, 2, tokens, block)
     one = array(bf16, tokens, block)
-    saved = (flat, one, two, two, two, two, array(f32, tokens, LANES), flat, array(f32, tokens, width), flat)
+    saved = (flat, one, two, two, two, two, array(f32, LANES, tokens), flat, array(f32, tokens, width), flat)
     wide = (array(f32, ranks, tokens, ff), array(bf16, ranks, tokens, ff))
     hidden = array(bf16, tokens, width)
-    after = (hidden, hidden, hidden, flat, one, two, two, two, two, array(f32, tokens, LANES), one)
+    after = (hidden, array(f32, 2, 4, width), hidden, hidden, flat, one, two, two, two, two, array(f32, LANES, tokens), one)
     dma = pltpu.SemaphoreType.DMA
     links = dma((len(HEAD_GROUPS), 3))
     out = pl.pallas_call(
@@ -1277,13 +1286,15 @@
             any_specs(2 * kinds)
             + vmem_specs(len(saved))
             + any_specs(2)
-            + vmem_specs(2)
+            + vmem_specs(3)
             + any_specs(1)
-            + vmem_specs(len(after) - 3)
+            + vmem_specs(len(after) - 4)
         ),
         scratch_shapes=[
             dma((2,)),
             dma((2,)),
+            dma((3,)),
+            pltpu.VMEM((tokens, LANES), f32),
             pltpu.VMEM((LINKED, tokens, tokens), f32),
             links,
             links,
@@ -1306,13 +1317,13 @@
         ),
         cost_estimate=pl.CostEstimate(flops=0, bytes_accessed=700_000_000, transcendentals=0),
         name="gather_and_forward",
-    )(place, rows_in, rows_cot, norms, *masters)
+    )(place, layer_in, cotangent, norms, *masters)
     weights, out = (out[:kinds], out[kinds:2 * kinds]), out[2 * kinds:]
     normed, query, own, along, beside, both, lse, attended, residual, second, slope, activated, *out = out
-    result, hidden, cotangent, *out = out
+    result, norms, hidden, cotangent, *out = out
     saved = (hidden, normed, query, [own, along, beside, both], attended, lse, residual, second, slope, activated)
     normed, query, own, along, beside, both, lse, attended = out
-    return weights, cotangent, saved, result, (normed, query, [own, along, beside, both], lse, attended)
+    return weights, norms, cotangent, saved, result, (normed, query, [own, along, beside, both], lse, attended)
 
 
 class Writer:
@@ -1357,25 +1368,20 @@
 def mlp_back_kernel(
     e_ref, slope_ref, g_ref, c_ref, ob_ref, r_ref, norm_ref, wo_ref, wf_ref, wp_ref,
     res_ref, att_ref, vec_ref, p_keep, p_give, f_keep, f_give, o_keep, o_give,
-    wo, wf, wp, slopes, gs, block_sems, pre, d_sec, branch, att_mem, p_slots, f_slots, o_slots, sems, p_sems, f_sems, o_sems,
+    wo, wf, wp, pre, d_sec, branch, att_mem, p_slots, f_slots, o_slots, sems, p_sems, f_sems, o_sems,
 ):
     ranks = wo.shape[0]
     loads = [block_loads(s, t, sems, i) for i, (s, t) in enumerate(((wp_ref, wp), (wf_ref, wf), (wo_ref, wo)))]
-    others = [block_loads(s, t, block_sems, i) for i, (s, t) in enumerate(((slope_ref, slopes), (g_ref, gs)))]
-    for b in range(ranks):
-        load_all([loads[0][b], others[0][b], others[1][b]])
-    for some in loads[1:]:
+    for some in loads:
         load_all(some)
     writer = Writer(p_slots, p_sems)
     rows, ff = c_ref.shape[2], g_ref.shape[2]
     width = e_ref.shape[1]
     for b in range(ranks):
         loads[0][b].wait()
-        others[0][b].wait()
-        others[1][b].wait()
-        pre[:, pl.ds(b * ff, ff)] = (dot_nt(e_ref[...], wp[b]) * slopes[b]).astype(bf16)
+        pre[:, pl.ds(b * ff, ff)] = (dot_nt(e_ref[...], wp[b]) * slope_ref[b]).astype(bf16)
         writer.put(
-            lambda s, b=b: product_into(s, gs.at[b], e_ref, width), p_keep.at[b], p_give.at[b]
+            lambda s, b=b: product_into(s, g_ref.at[b], e_ref, width), p_keep.at[b], p_give.at[b]
         )
     for b in range(ranks):
         loads[1][b].wait()
@@ -1421,15 +1427,12 @@
             jax.ShapeDtypeStruct((2, width), f32),
         )
         + tuple(half_rows(w) for w in (w_proj, w_proj, w_fc, w_fc, w_out, w_out)),
-        in_specs=vmem_specs(1) + any_specs(2) + vmem_specs(4) + any_specs(3),
+        in_specs=vmem_specs(7) + any_specs(3),
         out_specs=tuple(vmem_specs(3) + any_specs(6)),
         scratch_shapes=[
             pltpu.VMEM(w_out.shape, bf16),
             pltpu.VMEM(w_fc.shape, bf16),
             pltpu.VMEM(w_proj.shape, bf16),
-            pltpu.VMEM(slope.shape, f32),
-            pltpu.VMEM(activated.shape, bf16),
-            pltpu.SemaphoreType.DMA((2, ranks)),
             pltpu.VMEM((tokens, w_fc.shape[2]), bf16),
             pltpu.VMEM((tokens, width), f32),
             pltpu.VMEM((tokens, width), bf16),
@@ -1592,8 +1595,6 @@
     masters = (w_qkv[0], w_out[0], w_fc[0], w_proj[0])
     parts = (3, 1, ranks, 0)
     own_norms = jnp.concatenate([norm_gains[0], norm_biases[0]])
-    other_norms = swap_cores(own_norms)
-    norms = [per_core(own_norms, other_norms), per_core(other_norms, own_norms)]
 
     def attend(projected):
         normed, query, own_keys = projected
@@ -1610,10 +1611,13 @@
         return result, (hidden, normed, query, keys, attended, lse, residual, second, slope, activated)
 
     if linked:
-        weights, rows_cot, saved_first, first_out, attention = gather_and_forward(
-            place, layer_in[:, 0], cotangent[:, 0], jnp.stack(norms), masters, parts, ranks
+        weights, norms, rows_cot, saved_first, first_out, attention = gather_and_forward(
+            place, layer_in, cotangent, own_norms, masters, parts, ranks
         )
+        norms = (norms[0], norms[1])
     else:
+        other_norms = swap_cores(own_norms)
+        norms = (per_core(own_norms, other_norms), per_core(other_norms, own_norms))
         rows_in, rows_cot = own_rows(layer_in), own_rows(cotangent)
         weights = gather_weights(masters, parts, ranks)
         first_out, saved_first = forward(rows_in, 0, attend(project_qkv(rows_in, norms[0], weights[0][0])))
@@ -1629,11 +1633,11 @@
         kept, given = mlp_grads[0::2], mlp_grads[1::2]
         if linked:
             d_query, d_keys, sums, home = attention_backward(
-                place, query, d_att, lse.T, keys, kept, given, (6, 5, 3), layers, rows
+                place, query, d_att, lse, keys, kept, given, (4, 5, 2), layers, rows
             )
             d_pair = d_keys[0]
         else:
-            d_query, d_keys, _, home = attention_backward(place, query, d_att, lse.T, keys)
+            d_query, d_keys, _, home = attention_backward(place, query, d_att, lse, keys)
             d_pair = scatter_keys(d_keys)
             sums = plain_sums(kept, given)
         sent, vectors_one, *qkv_grads = qkv_back(d_query, d_pair, normed, hidden, d_residual, norms[layer], wqkv)

time: 786 us -> 762 us (0.969)
  Pallas kernels: 755 us -> 734 us
    pallas_call x2, Pallas kernels: 289 us -> 274 us  [attention_backward(): pl.pallas_call(functools.partial(attention_backward_kernel, blocks, reduc...]
  transfers between devices with their start and end apart: 1 -> 0, of which waited for: 0 -> 0; matrix products, arithmetic and copies ran while one was open for 1% -> 0% of each run, Pallas kernels for 0% -> 0%
where the time goes in v2:
time: 762 us; the launch traced here: 751 us
  Pallas kernels  734 us (96%)
  local copies, waits for them, and re-layouts  11.2 us (1%)
    pallas_call x2, Pallas kernels, attention_backward(): pl.pallas_call(functools.partial(attention_backward_kernel, blocks, reduc...  274 us
    pallas_call x1, Pallas kernels, gather_and_forward(): pl.pallas_call(functools.partial(forward_kernel, gather), out_shape=gathe...  251 us
    pallas_call x1, Pallas kernels, reduce_last(): pl.pallas_call(functools.partial(last_kernel, reduction, going, early, la...  100 us
    pallas_call x2, Pallas kernels, mlp_back(): pl.pallas_call(mlp_back_kernel, out_shape=(jax.ShapeDtypeStruct((tokens,...  55.9 us
    pallas_call x2, Pallas kernels, qkv_back(): pl.pallas_call(qkv_back_kernel, out_shape=(jax.ShapeDtypeStruct((tokens,...  25.6 us
    pallas_call x1, Pallas kernels, out_and_mlp(): pl.pallas_call(mlp_kernel, out_shape=(flat, jax.ShapeDtypeStruct((tokens,...  19.6 us

profile of v2, /device:TPU:0, one launch (start us, length us, event | category | flops | bytes accessed | tf_op | source)
XLA Modules:
  0.0 751.4 jit_solution(6420178952593783748)
XLA Ops:
  0.6 0.0 copy-start
  0.7 0.1 fusion
  0.8 1.2 constant_dynamic-slice_fusion
  2.0 0.0 copy-done
  2.0 0.0 copy-start.4
  2.0 0.6 gather_fusion
  2.7 1.2 pad_add_fusion.place
  3.9 1.3 pad_maximum_fusion.2.own_norms
  5.2 2.4 copy.22.in_ref
  7.6 0.0 copy-done.4
  7.6 1.4 copy.23.cot_in
  9.0 251.0 %gather_and_forward.1 = (bf16[4,288,3456]{2,1,0:T(8,128)(2,1)}, bf16[4,288,1120]{2,1,0:T(8,128)(2,1)}, bf16[4,288,4608]{2,1,0:T(8,128)(2,1)}, bf16[4,1152,1120]{...) custom-call(s32[5]{0:T(128)} %pad_add_fusion.place, ...), custom_call_target="tpu_custom_call" | custom-call | bytes 700000000 | tf_op jit(solution)/shard_map/gather_and_forward/pallas_call | solution.py:1281
  260.0 1.4 slice_bitcast_fusion
  261.3 19.6 %out_and_mlp.1 = (bf16[4,256,288]{2,1,0:T(8,128)(2,1)}, f32[256,1120]{1,0:T(8,128)}, bf16[4,256,288]{2,1,0:T(8,128)(2,1)}, f32[4,256,1152]{2,1,0:T(8,128)}, bf16...) custom-call(bf16[256,1152]{1,0:T(8,128)(2,1)} %get-tuple-element.98.o_ref, ...), custom_call_target="tpu_custom_call" | custom-call | flops 6020923392 | bytes 23519232 | tf_op jit(solution)/shard_map/out_and_mlp/pallas_call | solution.py:1074
  280.9 27.9 %mlp_backward.2 = (f32[256,1120]{1,0:T(8,128)}, bf16[256,1152]{1,0:T(8,128)(2,1)}, f32[2,1120]{1,0:T(2,128)}, bf16[4,576,1120]{2,1,0:T(8,128)(2,1)}, bf16[4,576,...) custom-call(bf16[256,1120]{1,0:T(8,128)(2,1)} %get-tuple-element.97., ...), custom_call_target="tpu_custom_call" | custom-call | flops 12041846784 | bytes 47038464 | tf_op jit(solution)/shard_map/mlp_backward/pallas_call | solution.py:1422
  308.8 136.9 %attention_backward.2 = (bf16[256,1152]{1,0:T(8,128)(2,1)}, bf16[2,256,1152]{2,1,0:T(8,128)(2,1)}, bf16[576,1120]{1,0:T(8,128)(2,1)}, bf16[144,4608]{1,0:T(8,128...) custom-call(s32[5]{0:T(128)} %pad_add_fusion.place, bf16[256,1152]{1,0:T(8,128)(2,1)} %get-tuple-element.96.q_ref, ...), custom_call_target="tpu_custom_call" | custom-call | flops 13421772800 | bytes 400000000 | tf_op jit(solution)/shard_map/attention_backward/pallas_call | solution.py:597
  445.7 12.8 %qkv_backward.2 = (bf16[256,1120]{1,0:T(8,128)(2,1)}, f32[2,1120]{1,0:T(2,128)}, bf16[4,144,3456]{2,1,0:T(8,128)(2,1)}, bf16[4,144,3456]{2,1,0:T(8,128)(2,1)}) custom-call(bf16[256,1152]{1,0:T(8,128)(2,1)} %get-tuple-element.123.dq_ref, bf16[2,256,1152]{2,1,0:T(8,128)(2,1)} %get-tuple-element.124.dkv_ref, bf16[4,256,288]{2,1,0:T(8,128)(2,1)} %get-tuple-element.125.a_ref, ...), custom_call_target="tpu_custom_call" | custom-call | flops 4076863488 | bytes 15925248 | tf_op jit(solution)/shard_map/qkv_backward/pallas_call | solution.py:1486
  458.5 28.0 %mlp_backward.3 = (f32[256,1120]{1,0:T(8,128)}, bf16[256,1152]{1,0:T(8,128)(2,1)}, f32[2,1120]{1,0:T(2,128)}, bf16[4,576,1120]{2,1,0:T(8,128)(2,1)}, bf16[4,576,...) custom-call(bf16[256,1120]{1,0:T(8,128)(2,1)} %get-tuple-element.130, ...), custom_call_target="tpu_custom_call" | custom-call | flops 12041846784 | bytes 47038464 | tf_op jit(solution)/shard_map/mlp_backward/pallas_call | solution.py:1422
  486.5 136.8 %attention_backward.3 = (bf16[256,1152]{1,0:T(8,128)(2,1)}, bf16[2,256,1152]{2,1,0:T(8,128)(2,1)}, bf16[576,1120]{1,0:T(8,128)(2,1)}, bf16[144,4608]{1,0:T(8,128...) custom-call(s32[5]{0:T(128)} %pad_add_fusion.place, bf16[256,1152]{1,0:T(8,128)(2,1)} %get-tuple-element.129.q_ref, ...), custom_call_target="tpu_custom_call" | custom-call | flops 13421772800 | bytes 400000000 | tf_op jit(solution)/shard_map/attention_backward/pallas_call | solution.py:597
  623.3 0.0 copy-start.2
  623.3 12.9 %qkv_backward.3 = (bf16[256,1120]{1,0:T(8,128)(2,1)}, f32[2,1120]{1,0:T(2,128)}, bf16[4,144,3456]{2,1,0:T(8,128)(2,1)}, bf16[4,144,3456]{2,1,0:T(8,128)(2,1)}) custom-call(bf16[256,1152]{1,0:T(8,128)(2,1)} %get-tuple-element.151.dq_ref, bf16[2,256,1152]{2,1,0:T(8,128)(2,1)} %get-tuple-element.152.dkv_ref, bf16[4,256,288]{2,1,0:T(8,128)(2,1)} %get-tuple-element.153.a_ref, ...), custom_call_target="tpu_custom_call" | custom-call | flops 4076863488 | bytes 15925248 | tf_op jit(solution)/shard_map/qkv_backward/pallas_call | solution.py:1486
  636.2 0.0 copy-start.8
  636.2 0.0 copy-start.6
  636.2 0.0 copy-start.7
  636.2 0.0 copy-start.5
  636.2 0.0 copy-done.2
  636.2 1.4 copy.24
  637.6 0.0 copy-done.8
  637.7 0.1 stack.42
  637.8 0.1 stack.44
  637.8 0.0 copy-done.6
  637.9 0.1 stack.47
  638.0 0.1 stack.49
  638.0 0.0 copy-done.7
  638.1 0.1 stack.43
  638.2 0.1 stack.45
  638.3 0.0 copy-done.5
  638.3 0.1 stack.48
  638.4 0.1 stack.50
  638.5 0.7 select_bitcast_fusion.1
  639.1 100.4 %reduce_last.1 = (bf16[144,3456]{1,0:T(8,128)(2,1)}, f32[4,280]{1,0:T(4,128)}, bf16[144,3456]{1,0:T(8,128)(2,1)}, bf16[2,256,1120]{2,1,0:T(8,128)(2,1)}, bf16[57...) custom-call(bf16[4,144,3456]{2,1,0:T(8,128)(2,1)} %get-tuple-element.128., ...), custom_call_target="tpu_custom_call" | custom-call | bytes 400000000 | tf_op jit(solution)/shard_map/reduce_last/pallas_call | solution.py:695
  739.5 0.0 copy-done.3
  739.6 1.4 select_bitcast_fusion
  741.0 0.0 copy-start.9
  741.0 1.4 copy.25
  742.4 0.0 copy-done.9
  742.4 0.6 slice_bitcast_fusion.2
  743.0 8.2 %finish.1 = (f32[1120,1120]{1,0:T(8,128)}, f32[280,4480]{1,0:T(8,128)}, f32[280,1120]{1,0:T(8,128)}, f32[280,3360]{1,0:T(8,128)}) custom-call(bf16[576,1120]{1,0:T(8,128)(2,1)} %get-tuple-element.165.refs_7_.refs_0_, bf16[144,4608]{1,0:T(8,128)(2,1)} %get-tuple-element.166.refs_8_.refs_1_, bf16[144,1120]{1,0:T(8,128)(2,1)} %get-tuple-element.167.refs_9_.refs_2_, ...), custom_call_target="tpu_custom_call" | custom-call | tf_op jit(solution)/shard_map/finish/pallas_call | solution.py:744
  (9 shorter events, 0.1 us)
Async XLA Ops:
  0.6 1.4 copy-start
  2.0 5.6 copy-start.4
  623.3 12.9 %copy-start.2 = (bf16[2,256,1120]{2,1,0:T(8,128)(2,1)S(1)}, bf16[2,256,1120]{2,1,0:T(8,128)(2,1)}, u32[]{:S(2)}) copy-start(bf16[2,256,1120]{2,1,0:T(8,128)(2,1)} %get-tuple-element.122) | copy-start | bytes 3440644
  636.2 1.5 copy-start.8
  636.2 1.6 copy-start.6
  636.2 1.8 copy-start.7
  636.2 2.0 copy-start.5
  639.1 100.4 %copy-start.3 = (bf16[2,256,1120]{2,1,0:T(8,128)(2,1)S(1)}, bf16[2,256,1120]{2,1,0:T(8,128)(2,1)}, u32[]{:S(2)}) copy-start(bf16[2,256,1120]{2,1,0:T(8,128)(2,1)} %get-tuple-element.172) | copy-start | bytes 3440644
  741.0 1.4 copy-start.9
  743.0 8.2 %copy-start.1 = (s32[4]{0:T(128)S(1)}, s32[4]{0:T(128)}, u32[]{:S(2)}) copy-start(s32[4]{0:T(128)} %param.13) | copy-start | bytes 52

commit v3 on v2

--- a/solution.py
+++ b/solution.py
@@ -983,12 +983,22 @@
     ]
 
 
-def split_columns(target, value):
+def split_columns(target, value, beside=None):
     ranks, _, padded = target.shape
     share = value.shape[1] // ranks
     target[...] = jnp.zeros(target.shape, target.dtype)
+    if beside is not None:
+        beside[...] = jnp.zeros(beside.shape, beside.dtype)
     for b in range(ranks):
-        target[b, :, pl.ds(0, share)] = value[:, b * share:(b + 1) * share]
+        part = value[:, b * share:(b + 1) * share]
+        target[b, :, pl.ds(0, share)] = part
+        if beside is not None:
+            beside[:, pl.ds(b * padded, share)] = part
+
+
+def one_product(beside, weight):
+    ranks, rows, columns = weight.shape
+    return dot_nn(beside[...], weight.reshape(ranks * rows, columns))
 
 
 def join_columns(target, parts):
@@ -1035,18 +1045,18 @@
 def mlp_kernel(
     o_ref, h_ref, norm_ref, wo_ref, wf_ref, wp_ref,
     ob_ref, r_ref, c_ref, slope_ref, g_ref, out_ref,
-    wo, wf, wp, sems,
+    wo, wf, wp, beside, sems,
 ):
     ranks = wo.shape[0]
     loads = [block_loads(s, t, sems, i) for i, (s, t) in enumerate(((wo_ref, wo), (wf_ref, wf), (wp_ref, wp)))]
     for some in loads:
         load_all(some)
-    split_columns(ob_ref, o_ref[:, pl.ds(0, h_ref.shape[1])])
+    split_columns(ob_ref, o_ref[:, pl.ds(0, h_ref.shape[1])], beside)
     for copy in loads[0]:
         copy.wait()
-    r_ref[...] = h_ref[...].astype(f32) + sum_of([dot_nn(ob_ref[b], wo[b]) for b in range(ranks)])
+    r_ref[...] = h_ref[...].astype(f32) + one_product(beside, wo[...])
     unit, _ = norm_parts(r_ref[...])
-    split_columns(c_ref, (unit * norm_ref[1:2] + norm_ref[3:4]).astype(bf16))
+    split_columns(c_ref, (unit * norm_ref[1:2] + norm_ref[3:4]).astype(bf16), beside)
     for copy in loads[1]:
         copy.wait()
     block = g_ref.shape[2]
@@ -1054,7 +1064,7 @@
 
     def columns(i, carry):
         at = pl.multiple_of(i * step, LANES)
-        pre = sum_of([dot_nn(c_ref[b], wf[b, :, pl.ds(at, step)]) for b in range(ranks)])
+        pre = one_product(beside, wf[:, :, pl.ds(at, step)])
         within = pl.ds(pl.multiple_of(lax.rem(i, 3) * step, LANES), step)
         g_ref[i // 3, :, within], slope_ref[i // 3, :, within] = gelu_parts(pre)
         return carry
@@ -1087,6 +1097,7 @@
             pltpu.VMEM(w_out.shape, bf16),
             pltpu.VMEM(w_fc.shape, bf16),
             pltpu.VMEM(w_proj.shape, bf16),
+            pltpu.VMEM((tokens, ranks * rows), bf16),
             pltpu.SemaphoreType.DMA((3, ranks)),
         ],
         compiler_params=pltpu.CompilerParams(vmem_limit_bytes=VMEM_LIMIT),
@@ -1104,12 +1115,12 @@
 
 
 FORWARD_ORDER = (
-    "f0", "f1", "s0", "f2", "t0", "s1", "40", "s2", "f3", "l0", "Q0", "f4", "S0", "t1", "A00", "f5", "s3",
-    "s4", "f6", "A01", "t2", "A02", "41", "s5", "f7", "A03", "t3", "43", "l1", "O", "s6", "42", "l2", "l3",
-    "W", "M", "B0", "t4", "B1", "B2", "44", "t5", "s7", "B3", "l4", "t6", "45", "Q1", "t7", "S1", "46", "47",
-    "l6", "l5", "A10", "l7", "A11", "A12", "A13",
+    "f0", "f1", "s0", "f2", "t0", "s1", "s2", "40", "f3", "t1", "l0", "f4", "Q0", "t2", "f5", "S0", "s4",
+    "s5", "41", "42", "s3", "l1", "O", "A00", "f6", "A01", "A02", "A03", "t3", "t5", "f7", "l2", "W", "43",
+    "t4", "M", "44", "s6", "l3", "V", "B0", "B1", "s7", "B2", "45", "l4", "B3", "l5", "t6", "Q1", "S1", "t7",
+    "46", "A10", "A11", "A12", "47", "l6", "A13", "l7",
 )
-FORWARD_OVER_SEQ = (3, 2, 3, 2, 3, 2, 2, 2)
+FORWARD_OVER_SEQ = (3, 3, 3, 2, 3, 1, 2, 2)
 
 
 def forward_kernel(gather, place, in_ref, cot_in, own_norms, *refs):
@@ -1118,9 +1129,10 @@
     whole, refs = refs[:2 * kinds], refs[2 * kinds:]
     (a_ref, q_ref, kv_ref, *others), refs = refs[:6], refs[6:]
     (lse_ref, ob_ref, r_ref, c_ref, slope_ref, g_ref, out_ref), refs = refs[:7], refs[7:]
-    (norm_ref, h_ref, cot_ref, next_a, next_q, next_kv, *next_others), refs = refs[:9], refs[9:]
+    (first_norms, second_norms, h_ref, cot_ref, next_a, next_q, next_kv, *next_others), refs = refs[:10], refs[10:]
     (next_lse, next_o), refs = refs[:2], refs[2:]
-    (rows_send, rows_recv, norm_sem, lse_mem, bias, links_send, links_recv, next_send, next_recv, total, columns_mem, rows_mem, wo, slopes, gs), refs = refs[:15], refs[15:]
+    (rows_send, rows_recv, norm_sem, lse_mem, bias, links_send, links_recv, next_send, next_recv), refs = refs[:9], refs[9:]
+    (total, beside, norm_ref, columns_mem, rows_mem, wo, slopes, gs), refs = refs[:8], refs[8:]
     (columns_sem, rows_sem, wo_sem, out_sem), refs = refs[:4], refs[4:]
     gather.bind(masters, whole, refs)
     gather.open()
@@ -1172,10 +1184,10 @@
         for part in range(2):
             load_all(load_columns(weight, part))
         unit, _ = norm_parts(hidden)
-        split_columns(a, (unit * norms[0:1] + norms[2:3]).astype(bf16))
+        split_columns(a, (unit * norms[0:1] + norms[2:3]).astype(bf16), beside)
         for part, target in enumerate((q, kv.at[0], kv.at[1])):
             wait_all(load_columns(weight, part))
-            target[...] = sum_of([dot_nn(a[b], columns_mem[part % 2, b]) for b in range(ranks)]).astype(bf16)
+            target[...] = one_product(beside, columns_mem[part % 2]).astype(bf16)
             if part == 0:
                 load_all(load_columns(weight, 2))
 
@@ -1195,7 +1207,7 @@
 
         def some_columns(i, carry):
             at = pl.ds(pl.multiple_of(i * third, LANES), third)
-            pre = sum_of([dot_nn(c_ref[k], columns_mem[slot, k, :, at]) for k in range(ranks)])
+            pre = one_product(beside, columns_mem[slot, :, :, at])
             gs[slot, :, at], slopes[slot, :, at] = gelu_parts(pre)
             return carry
 
@@ -1221,11 +1233,11 @@
 
     def middle():
         attention(0)[2]()
-        split_columns(ob_ref, next_o[:, pl.ds(0, h_ref.shape[1])])
+        split_columns(ob_ref, next_o[:, pl.ds(0, h_ref.shape[1])], beside)
         wait_all(out_loads)
-        r_ref[...] = h_ref[...].astype(f32) + sum_of([dot_nn(ob_ref[b], wo[b]) for b in range(ranks)])
+        r_ref[...] = h_ref[...].astype(f32) + one_product(beside, wo[...])
         unit, _ = norm_parts(r_ref[...])
-        split_columns(c_ref, (unit * norm_ref[0, 1:2] + norm_ref[0, 3:4]).astype(bf16))
+        split_columns(c_ref, (unit * norm_ref[0, 1:2] + norm_ref[0, 3:4]).astype(bf16), beside)
         total[...] = r_ref[...]
 
     def qkv(layer):
@@ -1233,6 +1245,8 @@
             rows_arrive(0)
             norms_here.wait()
             norms_there.wait()
+            first_norms[...] = norm_ref[0]
+            second_norms[...] = norm_ref[1]
             project(h_ref[...].astype(f32), norm_ref.at[0], whole[0], a_ref, q_ref, kv_ref)
             return
         for b in range(2, ranks):
@@ -1250,6 +1264,8 @@
         elif step == "W":
             for b in range(2):
                 load_all(load_columns(whole[2], b))
+        elif step == "V":
+            for b in range(2):
                 load_all(load_rows(whole[3], b))
         elif step[0] == "A":
             attention(int(step[1]))[1](int(step[2]))
@@ -1275,7 +1291,8 @@
     saved = (flat, one, two, two, two, two, array(f32, LANES, tokens), flat, array(f32, tokens, width), flat)
     wide = (array(f32, ranks, tokens, ff), array(bf16, ranks, tokens, ff))
     hidden = array(bf16, tokens, width)
-    after = (hidden, array(f32, 2, 4, width), hidden, hidden, flat, one, two, two, two, two, array(f32, LANES, tokens), one)
+    norm = array(f32, 4, width)
+    after = (hidden, norm, norm, hidden, hidden, flat, one, two, two, two, two, array(f32, LANES, tokens), one)
     dma = pltpu.SemaphoreType.DMA
     links = dma((len(HEAD_GROUPS), 3))
     out = pl.pallas_call(
@@ -1286,9 +1303,9 @@
             any_specs(2 * kinds)
             + vmem_specs(len(saved))
             + any_specs(2)
-            + vmem_specs(3)
+            + vmem_specs(4)
             + any_specs(1)
-            + vmem_specs(len(after) - 4)
+            + vmem_specs(len(after) - 5)
         ),
         scratch_shapes=[
             dma((2,)),
@@ -1301,6 +1318,8 @@
             links,
             links,
             pltpu.VMEM((tokens, width), f32),
+            pltpu.VMEM((tokens, ranks * rows), bf16),
+            pltpu.VMEM((2, 4, width), f32),
             pltpu.VMEM((2, ranks, rows, block), bf16),
             pltpu.VMEM((2, ff, width), bf16),
             pltpu.VMEM((ranks, rows, width), bf16),
@@ -1320,7 +1339,8 @@
     )(place, layer_in, cotangent, norms, *masters)
     weights, out = (out[:kinds], out[kinds:2 * kinds]), out[2 * kinds:]
     normed, query, own, along, beside, both, lse, attended, residual, second, slope, activated, *out = out
-    result, norms, hidden, cotangent, *out = out
+    result, *norms, hidden, cotangent = out[:5]
+    out = out[5:]
     saved = (hidden, normed, query, [own, along, beside, both], attended, lse, residual, second, slope, activated)
     normed, query, own, along, beside, both, lse, attended = out
     return weights, norms, cotangent, saved, result, (normed, query, [own, along, beside, both], lse, attended)
@@ -1614,7 +1634,6 @@
         weights, norms, rows_cot, saved_first, first_out, attention = gather_and_forward(
             place, layer_in, cotangent, own_norms, masters, parts, ranks
         )
-        norms = (norms[0], norms[1])
     else:
         other_norms = swap_cores(own_norms)
         norms = (per_core(own_norms, other_norms), per_core(other_norms, own_norms))

time: 762 us -> 746 us (0.979)
  Pallas kernels: 734 us -> 721 us
    pallas_call x1, Pallas kernels: 251 us -> 241 us  [gather_and_forward(): pl.pallas_call(functools.partial(forward_kernel, gather), out_shape=gathe...]
where the time goes in v3:
time: 746 us; the launch traced here: 737 us
  Pallas kernels  721 us (97%)
  local copies, waits for them, and re-layouts  9.87 us (1%)
    pallas_call x2, Pallas kernels, attention_backward(): pl.pallas_call(functools.partial(attention_backward_kernel, blocks, reduc...  271 us
    pallas_call x1, Pallas kernels, gather_and_forward(): pl.pallas_call(functools.partial(forward_kernel, gather), out_shape=gathe...  241 us
    pallas_call x1, Pallas kernels, reduce_last(): pl.pallas_call(functools.partial(last_kernel, reduction, going, early, la...  102 us
    pallas_call x2, Pallas kernels, mlp_back(): pl.pallas_call(mlp_back_kernel, out_shape=(jax.ShapeDtypeStruct((tokens,...  55.9 us
    pallas_call x2, Pallas kernels, qkv_back(): pl.pallas_call(qkv_back_kernel, out_shape=(jax.ShapeDtypeStruct((tokens,...  25.6 us
    pallas_call x1, Pallas kernels, out_and_mlp(): pl.pallas_call(mlp_kernel, out_shape=(flat, jax.ShapeDtypeStruct((tokens,...  17.8 us

profile of v3, /device:TPU:0, one launch (start us, length us, event | category | flops | bytes accessed | tf_op | source)
XLA Modules:
  0.0 737.0 jit_solution(10709933225076202723)
XLA Ops:
  0.6 0.0 copy-start
  0.7 0.1 fusion
  0.8 1.2 constant_dynamic-slice_fusion
  2.0 0.0 copy-done
  2.0 0.0 copy-start.4
  2.0 0.6 gather_fusion
  2.7 1.2 pad_add_fusion.place
  3.9 1.3 pad_maximum_fusion.2.own_norms
  5.2 2.4 copy.22.in_ref
  7.6 0.0 copy-done.4
  7.6 1.4 copy.23.cot_in
  9.0 241.0 %gather_and_forward.1 = (bf16[4,288,3456]{2,1,0:T(8,128)(2,1)}, bf16[4,288,1120]{2,1,0:T(8,128)(2,1)}, bf16[4,288,4608]{2,1,0:T(8,128)(2,1)}, bf16[4,1152,1120]{...) custom-call(s32[5]{0:T(128)} %pad_add_fusion.place, ...), custom_call_target="tpu_custom_call" | custom-call | bytes 700000000 | tf_op jit(solution)/shard_map/gather_and_forward/pallas_call | solution.py:1298
  250.0 17.8 %out_and_mlp.1 = (bf16[4,256,288]{2,1,0:T(8,128)(2,1)}, f32[256,1120]{1,0:T(8,128)}, bf16[4,256,288]{2,1,0:T(8,128)(2,1)}, f32[4,256,1152]{2,1,0:T(8,128)}, bf16...) custom-call(bf16[256,1152]{1,0:T(8,128)(2,1)} %get-tuple-element.99.o_ref, ...), custom_call_target="tpu_custom_call" | custom-call | flops 6020923392 | bytes 23519232 | tf_op jit(solution)/shard_map/out_and_mlp/pallas_call | solution.py:1084
  267.8 27.9 %mlp_backward.2 = (f32[256,1120]{1,0:T(8,128)}, bf16[256,1152]{1,0:T(8,128)(2,1)}, f32[2,1120]{1,0:T(2,128)}, bf16[4,576,1120]{2,1,0:T(8,128)(2,1)}, bf16[4,576,...) custom-call(bf16[256,1120]{1,0:T(8,128)(2,1)} %get-tuple-element.98., ...), custom_call_target="tpu_custom_call" | custom-call | flops 12041846784 | bytes 47038464 | tf_op jit(solution)/shard_map/mlp_backward/pallas_call | solution.py:1442
  295.7 135.5 %attention_backward.2 = (bf16[256,1152]{1,0:T(8,128)(2,1)}, bf16[2,256,1152]{2,1,0:T(8,128)(2,1)}, bf16[576,1120]{1,0:T(8,128)(2,1)}, bf16[144,4608]{1,0:T(8,128...) custom-call(s32[5]{0:T(128)} %pad_add_fusion.place, bf16[256,1152]{1,0:T(8,128)(2,1)} %get-tuple-element.97.q_ref, ...), custom_call_target="tpu_custom_call" | custom-call | flops 13421772800 | bytes 400000000 | tf_op jit(solution)/shard_map/attention_backward/pallas_call | solution.py:597
  431.2 12.8 %qkv_backward.2 = (bf16[256,1120]{1,0:T(8,128)(2,1)}, f32[2,1120]{1,0:T(2,128)}, bf16[4,144,3456]{2,1,0:T(8,128)(2,1)}, bf16[4,144,3456]{2,1,0:T(8,128)(2,1)}) custom-call(bf16[256,1152]{1,0:T(8,128)(2,1)} %get-tuple-element.124.dq_ref, bf16[2,256,1152]{2,1,0:T(8,128)(2,1)} %get-tuple-element.125.dkv_ref, bf16[4,256,288]{2,1,0:T(8,128)(2,1)} %get-tuple-element.126.a_ref, ...), custom_call_target="tpu_custom_call" | custom-call | flops 4076863488 | bytes 15925248 | tf_op jit(solution)/shard_map/qkv_backward/pallas_call | solution.py:1506
  444.0 28.0 %mlp_backward.3 = (f32[256,1120]{1,0:T(8,128)}, bf16[256,1152]{1,0:T(8,128)(2,1)}, f32[2,1120]{1,0:T(2,128)}, bf16[4,576,1120]{2,1,0:T(8,128)(2,1)}, bf16[4,576,...) custom-call(bf16[256,1120]{1,0:T(8,128)(2,1)} %get-tuple-element.131, ...), custom_call_target="tpu_custom_call" | custom-call | flops 12041846784 | bytes 47038464 | tf_op jit(solution)/shard_map/mlp_backward/pallas_call | solution.py:1442
  472.0 135.6 %attention_backward.3 = (bf16[256,1152]{1,0:T(8,128)(2,1)}, bf16[2,256,1152]{2,1,0:T(8,128)(2,1)}, bf16[576,1120]{1,0:T(8,128)(2,1)}, bf16[144,4608]{1,0:T(8,128...) custom-call(s32[5]{0:T(128)} %pad_add_fusion.place, bf16[256,1152]{1,0:T(8,128)(2,1)} %get-tuple-element.130.q_ref, ...), custom_call_target="tpu_custom_call" | custom-call | flops 13421772800 | bytes 400000000 | tf_op jit(solution)/shard_map/attention_backward/pallas_call | solution.py:597
  607.6 0.0 copy-start.2
  607.6 12.8 %qkv_backward.3 = (bf16[256,1120]{1,0:T(8,128)(2,1)}, f32[2,1120]{1,0:T(2,128)}, bf16[4,144,3456]{2,1,0:T(8,128)(2,1)}, bf16[4,144,3456]{2,1,0:T(8,128)(2,1)}) custom-call(bf16[256,1152]{1,0:T(8,128)(2,1)} %get-tuple-element.153.dq_ref, bf16[2,256,1152]{2,1,0:T(8,128)(2,1)} %get-tuple-element.154.dkv_ref, bf16[4,256,288]{2,1,0:T(8,128)(2,1)} %get-tuple-element.155.a_ref, ...), custom_call_target="tpu_custom_call" | custom-call | flops 4076863488 | bytes 15925248 | tf_op jit(solution)/shard_map/qkv_backward/pallas_call | solution.py:1506
  620.5 0.0 copy-start.8
  620.5 0.0 copy-start.6
  620.5 0.0 copy-start.7
  620.5 0.0 copy-start.5
  620.5 0.0 copy-done.2
  620.5 1.4 copy.24
  621.9 0.0 copy-done.8
  622.0 0.1 stack.42
  622.1 0.1 stack.44
  622.1 0.0 copy-done.6
  622.2 0.1 stack.47
  622.3 0.1 stack.49
  622.4 0.0 copy-done.7
  622.4 0.1 stack.43
  622.5 0.1 stack.45
  622.6 0.0 copy-done.5
  622.6 0.1 stack.48
  622.7 0.1 stack.50
  622.8 0.7 select_bitcast_fusion.1
  623.4 101.7 %reduce_last.1 = (bf16[144,3456]{1,0:T(8,128)(2,1)}, f32[4,280]{1,0:T(4,128)}, bf16[144,3456]{1,0:T(8,128)(2,1)}, bf16[2,256,1120]{2,1,0:T(8,128)(2,1)}, bf16[57...) custom-call(bf16[4,144,3456]{2,1,0:T(8,128)(2,1)} %get-tuple-element.129., ...), custom_call_target="tpu_custom_call" | custom-call | bytes 400000000 | tf_op jit(solution)/shard_map/reduce_last/pallas_call | solution.py:695
  725.2 0.0 copy-done.3
  725.2 1.4 select_bitcast_fusion
  726.6 0.0 copy-start.9
  726.6 1.4 copy.25
  728.0 0.0 copy-done.9
  728.0 0.6 slice_bitcast_fusion
  728.6 8.2 %finish.1 = (f32[1120,1120]{1,0:T(8,128)}, f32[280,4480]{1,0:T(8,128)}, f32[280,1120]{1,0:T(8,128)}, f32[280,3360]{1,0:T(8,128)}) custom-call(bf16[576,1120]{1,0:T(8,128)(2,1)} %get-tuple-element.167.refs_7_.refs_0_, bf16[144,4608]{1,0:T(8,128)(2,1)} %get-tuple-element.168.refs_8_.refs_1_, bf16[144,1120]{1,0:T(8,128)(2,1)} %get-tuple-element.169.refs_9_.refs_2_, ...), custom_call_target="tpu_custom_call" | custom-call | tf_op jit(solution)/shard_map/finish/pallas_call | solution.py:744
  736.8 0.0 copy-done.1
  (8 shorter events, 0.1 us)
Async XLA Ops:
  0.6 1.4 copy-start
  2.0 5.6 copy-start.4
  607.6 12.9 %copy-start.2 = (bf16[2,256,1120]{2,1,0:T(8,128)(2,1)S(1)}, bf16[2,256,1120]{2,1,0:T(8,128)(2,1)}, u32[]{:S(2)}) copy-start(bf16[2,256,1120]{2,1,0:T(8,128)(2,1)} %get-tuple-element.123) | copy-start | bytes 3440644
  620.5 1.5 copy-start.8
  620.5 1.6 copy-start.6
  620.5 1.8 copy-start.7
  620.5 2.0 copy-start.5
  623.4 101.7 %copy-start.3 = (bf16[2,256,1120]{2,1,0:T(8,128)(2,1)S(1)}, bf16[2,256,1120]{2,1,0:T(8,128)(2,1)}, u32[]{:S(2)}) copy-start(bf16[2,256,1120]{2,1,0:T(8,128)(2,1)} %get-tuple-element.174) | copy-start | bytes 3440644
  726.6 1.4 copy-start.9
  728.6 8.2 %copy-start.1 = (s32[4]{0:T(128)S(1)}, s32[4]{0:T(128)}, u32[]{:S(2)}) copy-start(s32[4]{0:T(128)} %param.13) | copy-start | bytes 52
